TPU v7x, 32 devices: a whole 2x2x4 slice. The times are simulated.
32 devices in a mesh: dp: 8 (over z, y), mp: 4 (over x, core).
Axes of the slice: x: 2, y: 2, z: 4, core: 2. Of those that a mesh axis runs over, the one named last changes fastest.
Arguments:
- media: bfloat16 [16, 1280, 1024], P('dp'), may hold values from -6 to 6
- latents: bfloat16 [16, 64, 1024], P('dp'), may hold values from -6 to 6
- cotangent: bfloat16 [16, 64, 1024], P('dp'), may hold values from -6 to 6
- image_counts: int32 [16], P('dp'), may hold values from 1 to 5
- query_matrix: bfloat16 [1024, 512], P('dp', 'mp'), may hold values from -0.1875 to 0.1875
- k_weight: bfloat16 [1024, 512], P('dp', 'mp'), may hold values from -0.1875 to 0.1875
- v_weight: bfloat16 [1024, 512], P('dp', 'mp'), may hold values from -0.1875 to 0.1875
- output_projection_weight: bfloat16 [512, 1024], P('mp', 'dp'), may hold values from -6 to 6
- up_projection_weight: bfloat16 [1024, 4096], P('dp', 'mp'), may hold values from -0.1875 to 0.1875
- down_projection_weight: bfloat16 [4096, 1024], P('mp', 'dp'), may hold values from -0.09375 to 0.09375
- media_gain: bfloat16 [1024], P('dp'), may hold values from 0.5 to 1.5
- media_bias: bfloat16 [1024], P('dp'), may hold values from -3 to 3
- latent_gain: bfloat16 [1024], P('dp'), may hold values from 0.5 to 1.5
- latent_bias: bfloat16 [1024], P('dp'), may hold values from -3 to 3
- ff_gain: bfloat16 [1024], P('dp'), may hold values from 0.5 to 1.5
- ff_bias: bfloat16 [1024], P('dp'), may hold values from -3 to 3
Outputs:
- latents_out: bfloat16 [16, 64, 1024], P('dp')
- media_grad: bfloat16 [16, 1280, 1024], P('dp')
- latent_grad: bfloat16 [16, 64, 1024], P('dp')
- query_weight_grad: float32 [1024, 512], P('dp', 'mp')
- k_grad: float32 [1024, 512], P('dp', 'mp')
- v_grad: float32 [1024, 512], P('dp', 'mp')
- output_projection_grad: float32 [512, 1024], P('mp', 'dp')
- up_projection_grad: float32 [1024, 4096], P('dp', 'mp')
- down_projection_grad: float32 [4096, 1024], P('mp', 'dp')
- media_gain_grad: float32 [1024], P('dp')
- media_bias_grad: float32 [1024], P('dp')
- latent_gain_grad: float32 [1024], P('dp')
- latent_bias_grad: float32 [1024], P('dp')
- ff_gain_grad: float32 [1024], P('dp')
- ff_bias_grad: float32 [1024], P('dp')
Inputs may be any that keep to these rules, and one draw needn't show every extreme that they name: image_counts[b] is the number of images of sample b; they fill its first image slots.
All inputs are finite; a program needn't handle non-finite values.
Results may differ from a plain program's by a relative error of at most 0.017.
Values may be sent and summed in bfloat16 or wider, within the bound.
A program may use at most 128 MiB of HBM per device.

v0:
```python
import jax
import jax.numpy as jnp
from jax import lax
from jax.sharding import PartitionSpec as P

HEAD = 64
PATCH = 256
MB = 2
SB = 1


def layer_norm(inputs, gain, bias):
    center = inputs - jnp.mean(inputs, axis=-1, keepdims=True)
    spread = jnp.mean(center * center, axis=-1, keepdims=True)
    return center * lax.rsqrt(spread + 1e-05) * gain + bias


def gelu_exact(inputs):
    return jax.nn.gelu(inputs, approximate=False)


def add_tuples(left, right):
    return tuple((first + second for first, second in zip(left, right)))


def micro_step(gathered, media, latents, cotangent, counts):
    (
        query_matrix,
        k_weight,
        v_weight,
        output_projection_weight,
        up_projection_weight,
        down_projection_weight,
        media_gain,
        media_bias,
        latent_gain,
        latent_bias,
        ff_gain,
        ff_bias,
    ) = gathered
    samples = media.shape[0]
    media_len = media.shape[1]
    latent_len = latents.shape[1]
    keys_len = media_len + latent_len
    span = query_matrix.shape[1]
    local_heads = span // HEAD
    wide_rows = jnp.float32
    key_matrix = jnp.concatenate([k_weight, v_weight], axis=1)
    latent_full = latents.astype(wide_rows)
    latent_norm32, latent_pull = jax.vjp(
        layer_norm, latent_full, latent_gain.astype(wide_rows), latent_bias.astype(wide_rows)
    )
    latent_normed_rows = latent_norm32.astype(jnp.bfloat16)
    media_norm32, media_pull = jax.vjp(
        layer_norm,
        media.astype(wide_rows),
        media_gain.astype(wide_rows),
        media_bias.astype(wide_rows),
    )
    media_norm = media_norm32.astype(jnp.bfloat16)
    media_kv = jnp.einsum(
        "snd,dh->snh", media_norm, key_matrix, preferred_element_type=wide_rows
    ).astype(jnp.bfloat16)
    query_rows = jnp.einsum(
        "gjm,mu->gju", latent_normed_rows, query_matrix, preferred_element_type=wide_rows
    ).astype(jnp.bfloat16)
    latent_kv = jnp.einsum(
        "gjm,mu->gju", latent_normed_rows, key_matrix, preferred_element_type=wide_rows
    ).astype(jnp.bfloat16)
    both_kv = jnp.concatenate([media_kv, latent_kv], axis=1)
    head_queries = query_rows.reshape(samples, latent_len, local_heads, HEAD)
    head_keys = both_kv[:, :, :span].reshape(samples, keys_len, local_heads, HEAD)
    head_values = both_kv[:, :, span:].reshape(samples, keys_len, local_heads, HEAD)
    places = jnp.arange(keys_len)
    valid = jnp.logical_or(places[None, :] // PATCH < counts[:, None], places[None, :] >= media_len)

    def scores_of():
        raw = (
            jnp.einsum("slhe,snhe->shln", head_queries, head_keys, preferred_element_type=wide_rows)
            * 0.125
        )
        return jnp.where(valid[:, None, None, :], raw, -1e30)

    scores = scores_of()
    row_max = jnp.max(scores, axis=-1, keepdims=True)
    logsum = row_max + jnp.log(jnp.sum(jnp.exp(scores - row_max), axis=-1, keepdims=True))
    attend_low = jnp.exp(scores - logsum).astype(jnp.bfloat16)
    mixed_rows = jnp.einsum(
        "shln,snhe->slhe", attend_low, head_values, preferred_element_type=wide_rows
    )
    mixed_rows = mixed_rows.reshape(samples, latent_len, span).astype(jnp.bfloat16)
    attn_out = lax.psum(
        jnp.einsum(
            "rwa,ax->rwx", mixed_rows, output_projection_weight, preferred_element_type=wide_rows
        ),
        "mp",
    )
    middle = latent_full + attn_out
    hidden32, ff_pull = jax.vjp(
        layer_norm, middle, ff_gain.astype(wide_rows), ff_bias.astype(wide_rows)
    )
    hidden_rows = hidden32.astype(jnp.bfloat16)
    inner_rows = jnp.einsum(
        "qab,bo->qao", hidden_rows, up_projection_weight, preferred_element_type=wide_rows
    )
    active32, gelu_pull = jax.vjp(gelu_exact, inner_rows)
    active_units = active32.astype(jnp.bfloat16)
    ff_out = lax.psum(
        jnp.einsum(
            "pye,ej->pyj", active_units, down_projection_weight, preferred_element_type=wide_rows
        ).astype(jnp.bfloat16),
        "mp",
    ).astype(jnp.float32)
    result = (middle + ff_out).astype(jnp.bfloat16)
    down_projection_grad = jnp.einsum(
        "kje,kju->eu", active_units, cotangent, preferred_element_type=wide_rows
    )
    active_units_grad = jnp.einsum(
        "jvw,ow->jvo", cotangent, down_projection_weight, preferred_element_type=wide_rows
    )
    (inner_grad,) = gelu_pull(active_units_grad)
    inner_rows_reduced = inner_grad.astype(jnp.bfloat16)
    up_projection_grad = jnp.einsum(
        "imw,imk->wk", hidden_rows, inner_rows_reduced, preferred_element_type=wide_rows
    )
    hidden_grad = lax.psum(
        jnp.einsum(
            "xvm,nm->xvn",
            inner_rows_reduced,
            up_projection_weight,
            preferred_element_type=wide_rows,
        ).astype(jnp.bfloat16),
        "mp",
    ).astype(jnp.float32)
    middle_part, ff_gain_grad, ff_bias_grad = ff_pull(hidden_grad)
    middle_grad = cotangent.astype(wide_rows) + middle_part
    middle_rows_reduced = middle_grad.astype(jnp.bfloat16)
    output_projection_grad = jnp.einsum(
        "gfb,gfw->bw", mixed_rows, middle_rows_reduced, preferred_element_type=wide_rows
    )
    mixed_grad = jnp.einsum(
        "kzw,nw->kzn",
        middle_rows_reduced,
        output_projection_weight,
        preferred_element_type=wide_rows,
    ).astype(jnp.bfloat16)
    mixed_grad = mixed_grad.reshape(samples, latent_len, local_heads, HEAD)
    attend = jnp.exp(scores_of() - logsum)
    attend_grad = jnp.einsum(
        "slhe,snhe->shln", mixed_grad, head_values, preferred_element_type=wide_rows
    )
    score_grad = attend * (attend_grad - jnp.sum(attend * attend_grad, axis=-1, keepdims=True))
    score_grad = score_grad.astype(jnp.bfloat16)
    query_rows_grad = (
        jnp.einsum("shln,snhe->slhe", score_grad, head_keys, preferred_element_type=wide_rows)
        * 0.125
    )
    query_rows_grad = query_rows_grad.astype(jnp.bfloat16).reshape(samples, latent_len, span)
    key_grad = (
        jnp.einsum("shln,slhe->snhe", score_grad, head_queries, preferred_element_type=wide_rows)
        * 0.125
    )
    key_grad = key_grad.astype(jnp.bfloat16).reshape(samples, keys_len, span)
    value_grad = jnp.einsum(
        "shln,slhe->snhe", attend_low, mixed_grad, preferred_element_type=wide_rows
    )
    value_grad = value_grad.astype(jnp.bfloat16).reshape(samples, keys_len, span)
    kv_grad = jnp.concatenate([key_grad, value_grad], axis=2)
    media_kv_grad = kv_grad[:, :media_len]
    latent_key_value_grad = kv_grad[:, media_len:]
    query_weight_grad = jnp.einsum(
        "cbi,cbu->iu", latent_normed_rows, query_rows_grad, preferred_element_type=wide_rows
    )
    latent_wgrad = jnp.einsum(
        "cbi,cbu->iu", latent_normed_rows, latent_key_value_grad, preferred_element_type=wide_rows
    )
    latent_portion = jnp.einsum(
        "kwt,gt->kwg", query_rows_grad, query_matrix, preferred_element_type=wide_rows
    )
    latent_portion = latent_portion + jnp.einsum(
        "kwt,gt->kwg", latent_key_value_grad, key_matrix, preferred_element_type=wide_rows
    )
    media_part = jnp.einsum(
        "snh,dh->snd", media_kv_grad, key_matrix, preferred_element_type=wide_rows
    )
    media_wgrad = jnp.einsum(
        "snd,snh->dh", media_norm, media_kv_grad, preferred_element_type=wide_rows
    )
    kv_weight_grad = media_wgrad + latent_wgrad
    media_sum, latent_sum = (
        lax.psum(media_part.astype(jnp.bfloat16), "mp").astype(jnp.float32),
        lax.psum(latent_portion.astype(jnp.bfloat16), "mp").astype(jnp.float32),
    )
    media_back, media_gain_grad, media_bias_grad = media_pull(media_sum)
    media_out = media_back.astype(jnp.bfloat16)
    latent_back, latent_gain_grad, latent_bias_grad = latent_pull(latent_sum)
    latent_grad = middle_grad + latent_back
    grads = (
        query_weight_grad,
        kv_weight_grad[:, :span],
        kv_weight_grad[:, span:],
        output_projection_grad,
        up_projection_grad,
        down_projection_grad,
        media_gain_grad,
        media_bias_grad,
        latent_gain_grad,
        latent_bias_grad,
        ff_gain_grad,
        ff_bias_grad,
    )
    return (result, media_out, latent_grad.astype(jnp.bfloat16), grads)


def local(
    media,
    latents,
    cotangent,
    image_counts,
    query_matrix,
    k_weight,
    v_weight,
    output_projection_weight,
    up_projection_weight,
    down_projection_weight,
    media_gain,
    media_bias,
    latent_gain,
    latent_bias,
    ff_gain,
    ff_bias,
):
    results = []
    media_grads = []
    latent_grads = []
    totals = ()
    for micro_index in range(MB):
        gathered = (
            lax.all_gather(query_matrix, "dp", axis=0, tiled=True),
            lax.all_gather(k_weight, "dp", axis=0, tiled=True),
            lax.all_gather(v_weight, "dp", axis=0, tiled=True),
            lax.all_gather(output_projection_weight, "dp", axis=1, tiled=True),
            lax.all_gather(up_projection_weight, "dp", axis=0, tiled=True),
            lax.all_gather(down_projection_weight, "dp", axis=1, tiled=True),
            lax.all_gather(media_gain, "dp", axis=0, tiled=True),
            lax.all_gather(media_bias, "dp", axis=0, tiled=True),
            lax.all_gather(latent_gain, "dp", axis=0, tiled=True),
            lax.all_gather(latent_bias, "dp", axis=0, tiled=True),
            lax.all_gather(ff_gain, "dp", axis=0, tiled=True),
            lax.all_gather(ff_bias, "dp", axis=0, tiled=True),
        )
        lower = micro_index * SB
        upper = lower + SB
        result, media_back, latent_back, grads = micro_step(
            gathered,
            media[lower:upper],
            latents[lower:upper],
            cotangent[lower:upper],
            image_counts[lower:upper],
        )
        grads = (
            lax.psum_scatter(grads[0], "dp", scatter_dimension=0, tiled=True),
            lax.psum_scatter(grads[1], "dp", scatter_dimension=0, tiled=True),
            lax.psum_scatter(grads[2], "dp", scatter_dimension=0, tiled=True),
            lax.psum_scatter(grads[3], "dp", scatter_dimension=1, tiled=True),
            lax.psum_scatter(grads[4], "dp", scatter_dimension=0, tiled=True),
            lax.psum_scatter(grads[5], "dp", scatter_dimension=1, tiled=True),
            lax.psum_scatter(grads[6], "dp", scatter_dimension=0, tiled=True),
            lax.psum_scatter(grads[7], "dp", scatter_dimension=0, tiled=True),
            lax.psum_scatter(grads[8], "dp", scatter_dimension=0, tiled=True),
            lax.psum_scatter(grads[9], "dp", scatter_dimension=0, tiled=True),
            lax.psum_scatter(grads[10], "dp", scatter_dimension=0, tiled=True),
            lax.psum_scatter(grads[11], "dp", scatter_dimension=0, tiled=True),
        )
        totals = grads if micro_index == 0 else add_tuples(totals, grads)
        results.append(result)
        media_grads.append(media_back)
        latent_grads.append(latent_back)
    return (
        jnp.concatenate(results, axis=0),
        jnp.concatenate(media_grads, axis=0),
        jnp.concatenate(latent_grads, axis=0),
        totals[0],
        totals[1],
        totals[2],
        totals[3],
        totals[4],
        totals[5],
        totals[6],
        totals[7],
        totals[8],
        totals[9],
        totals[10],
        totals[11],
    )


def solution(mesh):
    placed = (
        P("dp", None, None),
        P("dp", None, None),
        P("dp", None, None),
        P("dp"),
        P("dp", "mp"),
        P("dp", "mp"),
        P("dp", "mp"),
        P("mp", "dp"),
        P("dp", "mp"),
        P("mp", "dp"),
        P("dp"),
        P("dp"),
        P("dp"),
        P("dp"),
        P("dp"),
        P("dp"),
    )
    return jax.shard_map(
        local,
        mesh=mesh,
        in_specs=placed,
        out_specs=(
            P("dp", None, None),
            P("dp", None, None),
            P("dp", None, None),
            P("dp", "mp"),
            P("dp", "mp"),
            P("dp", "mp"),
            P("mp", "dp"),
            P("dp", "mp"),
            P("mp", "dp"),
            P("dp"),
            P("dp"),
            P("dp"),
            P("dp"),
            P("dp"),
            P("dp"),
        ),
        check_vma=False,
    )
```

profile of v0, /device:TPU:0, one launch (start us, length us, event | category | flops | bytes accessed | tf_op | source)
XLA Modules:
  0.0 845.9 jit_solution(17543312719799933101)
XLA Ops:
  11.0 22.3 %all-gather.2 = bf16[8,1,128]{2,1,0:T(2,128)(2,1)S(1)} all-gather(bf16[1,1,128]{2,1,0:T(2,128)(2,1)} %bitcast.285), channel_id=1, replica_groups=mesh['dp'=8,'mp'=4] {'dp'}, dimensions={0}, use_global_device_ids=true | all-gather | bytes 2304 | tf_op jit(solution)/shard_map/all_gather | solution.py:247
  33.3 16.4 %all-gather.3 = bf16[8,1,128]{2,1,0:T(2,128)(2,1)S(1)} all-gather(bf16[1,1,128]{2,1,0:T(2,128)(2,1)} %bitcast.286), channel_id=1, replica_groups=mesh['dp'=8,'mp'=4] {'dp'}, dimensions={0}, use_global_device_ids=true | all-gather | bytes 2304 | tf_op jit(solution)/shard_map/all_gather | solution.py:248
  49.7 31.0 %all_gather.54 = bf16[1024,128]{1,0:T(8,128)(2,1)S(1)} all-gather(bf16[128,128]{1,0:T(8,128)(2,1)} %param.20), channel_id=1, replica_groups=mesh['dp'=8,'mp'=4] {'dp'}, dimensions={0}, use_global_device_ids=true | all-gather | bytes 294912 | tf_op jit(solution)/shard_map/all_gather | solution.py:239
  83.1 31.0 %all_gather.50 = bf16[1024,128]{1,0:T(8,128)(2,1)S(1)} all-gather(bf16[128,128]{1,0:T(8,128)(2,1)} %param.21), channel_id=1, replica_groups=mesh['dp'=8,'mp'=4] {'dp'}, dimensions={0}, use_global_device_ids=true | all-gather | bytes 294912 | tf_op jit(solution)/shard_map/all_gather | solution.py:240
  114.1 31.0 %all_gather.51 = bf16[1024,128]{1,0:T(8,128)(2,1)S(1)} all-gather(bf16[128,128]{1,0:T(8,128)(2,1)} %param.22), channel_id=1, replica_groups=mesh['dp'=8,'mp'=4] {'dp'}, dimensions={0}, use_global_device_ids=true | all-gather | bytes 294912 | tf_op jit(solution)/shard_map/all_gather | solution.py:241
  149.6 18.0 %all-gather = bf16[8,1,128]{2,1,0:T(2,128)(2,1)S(1)} all-gather(bf16[1,1,128]{2,1,0:T(2,128)(2,1)S(1)} %bitcast.287), channel_id=1, replica_groups=mesh['dp'=8,'mp'=4] {'dp'}, dimensions={0}, use_global_device_ids=true | all-gather | bytes 2304 | tf_op jit(solution)/shard_map/all_gather | solution.py:245
  167.6 16.3 %all-gather.1 = bf16[8,1,128]{2,1,0:T(2,128)(2,1)S(1)} all-gather(bf16[1,1,128]{2,1,0:T(2,128)(2,1)S(1)} %bitcast.288), channel_id=1, replica_groups=mesh['dp'=8,'mp'=4] {'dp'}, dimensions={0}, use_global_device_ids=true | all-gather | bytes 2304 | tf_op jit(solution)/shard_map/all_gather | solution.py:246
  187.8 26.4 %all_gather.55 = bf16[128,1024]{1,0:T(8,128)(2,1)S(1)} all-gather(bf16[128,128]{1,0:T(8,128)(2,1)S(1)} %copy-done.78), channel_id=1, replica_groups=mesh['dp'=8,'mp'=4] {'dp'}, dimensions={1}, use_global_device_ids=true | all-gather | bytes 294912 | tf_op jit(solution)/shard_map/all_gather | solution.py:242
  214.2 4.9 fusion.26
  229.6 16.4 %all-gather.4 = bf16[8,1,128]{2,1,0:T(2,128)(2,1)S(1)} all-gather(bf16[1,1,128]{2,1,0:T(2,128)(2,1)S(1)} %bitcast.289), channel_id=1, replica_groups=mesh['dp'=8,'mp'=4] {'dp'}, dimensions={0}, use_global_device_ids=true | all-gather | bytes 2304 | tf_op jit(solution)/shard_map/all_gather | solution.py:249
  246.6 18.2 %all-gather.5 = bf16[8,1,128]{2,1,0:T(2,128)(2,1)S(1)} all-gather(bf16[1,1,128]{2,1,0:T(2,128)(2,1)S(1)} %bitcast.290), channel_id=1, replica_groups=mesh['dp'=8,'mp'=4] {'dp'}, dimensions={0}, use_global_device_ids=true | all-gather | bytes 2304 | tf_op jit(solution)/shard_map/all_gather | solution.py:250
  268.6 8.8 %all-gather.9.cloned.1.call-done = bf16[1024,1024]{1,0:T(8,128)(2,1)} async-done(((bf16[128,1024]{1,0:T(8,128)(2,1)}), bf16[1024,1024]{1,0:T(8,128)(2,1)}) %all-gather.9.cloned.1.call-update) | async-done | bytes 2097168 | tf_op jit(solution)/shard_map/all_gather | solution.py:243
  280.5 47.8 %all-gather.11.cloned.1.call-done = bf16[1024,1024]{1,0:T(8,128)(2,1)} async-done(((bf16[1024,128]{1,0:T(8,128)(2,1)}), bf16[1024,1024]{1,0:T(8,128)(2,1)}) %all-gather.11.cloned.1.call-update) | async-done | bytes 2097168 | tf_op jit(solution)/shard_map/all_gather | solution.py:244
  337.4 3.4 fusion.38
  342.5 25.3 %all-reduce.18.cloned.1.call-done = (bf16[1,64,1024]{2,1,0:T(8,128)(2,1)}, bf16[1,64,1024]{2,1,0:T(8,128)(2,1)}) async-done(((bf16[1,64,1024]{2,1,0:T(8,128)(2,1)}, bf16[1,64,1024]{2,1,0:T(8,128)(2,1)}), (bf16[1,64,1024]{2,1,0:T(8,128)(2,1)}, bf16[1,64,1024]{2,1,0:T(8,128)(2,1)})) %all-reduce.18.cloned.1.call-update) | async-done | bytes 262160 | tf_op jit(solution)/shard_map/psum | solution.py:126
  411.8 91.3 %all-reduce.16.cloned.1.call-done = (bf16[1,64,1024]{2,1,0:T(8,128)(2,1)}, bf16[1,64,1024]{2,1,0:T(8,128)(2,1)}, bf16[1,1280,1024]{2,1,0:T(8,128)(2,1)}, bf16[1,...) async-done(((bf16[1,64,1024]{2,1,0:T(8,128)(2,1)}, bf16[1,64,1024]{2,1,0:T(8,128)(2,1)}, bf16[1,1280,1024]{2,1,0:T(8,128)(2,1)}, ...) | async-done | bytes 5767184 | tf_op jit(solution)/shard_map/psum | solution.py:108
  507.7 6.0 fusion.17
  515.5 6.8 fusion.20
  522.9 38.6 %all-reduce.6 = (f32[1024]{0:T(1024)}, f32[1024]{0:T(1024)}, f32[1024]{0:T(1024)}, f32[1024]{0:T(1024)}, f32[1024]{0:T(1024)}, /*index=5*/f32[1024]{0:T(1024)}) all-reduce(f32[1024]{0:T(1024)} %add.324, f32[1024]{0:T(1024)} %add.325, f32[1024]{0:T(1024)} %add.326, f32[1024]{0:T(1024)} %add.327, ...), channel_id=20, replica_groups=mesh['dp'=8,'mp'=4] {'dp'}, use_global_device_ids=true, to_apply=%region_53.54.clone | all-reduce | flops 6144 | bytes 49152
  576.5 6.5 add_convert_fusion.1
  585.9 4.4 reduce-scatter.13.cloned.1.call-done
  590.3 64.9 %reduce-scatter.7.cloned.1.call-done = f32[128,128]{1,0:T(8,128)} async-done(((f32[1024,128]{1,0:T(8,128)}), f32[128,128]{1,0:T(8,128)}) %reduce-scatter.7.cloned.1.call-update) | async-done | bytes 65552 | tf_op jit(solution)/shard_map/reduce_scatter | solution.py:262
  655.3 91.4 %reduce-scatter.15.cloned.1.call-done = f32[128,1024]{1,0:T(8,128)} async-done(((f32[1024,1024]{1,0:T(8,128)}), f32[128,1024]{1,0:T(8,128)}) %reduce-scatter.15.cloned.1.call-update) | async-done | bytes 524304 | tf_op jit(solution)/shard_map/reduce_scatter | solution.py:266
  746.7 92.2 %reduce-scatter.17.cloned.1.call-done = f32[1024,128]{1,0:T(8,128)} async-done(((f32[1024,1024]{1,0:T(8,128)}), f32[1024,128]{1,0:T(8,128)}) %reduce-scatter.17.cloned.1.call-update) | async-done | bytes 524304 | tf_op jit(solution)/shard_map/reduce_scatter | solution.py:267
  (416 shorter events, 108.7 us)
Async XLA Ops:
  8.0 139.7 %copy-start.110 = (s32[2]{0:T(128)S(1)}, s32[2]{0:T(128)}, u32[]{:S(2)}) copy-start(s32[2]{0:T(128)} %param.19) | copy-start | bytes 28
  8.0 141.6 %copy-start.121 = (bf16[128]{0:T(256)(128)(2,1)S(1)}, bf16[128]{0:T(256)(128)(2,1)}, u32[]{:S(2)}) copy-start(bf16[128]{0:T(256)(128)(2,1)} %param.26) | copy-start | bytes 772
  8.0 159.6 %copy-start.122 = (bf16[128]{0:T(256)(128)(2,1)S(1)}, bf16[128]{0:T(256)(128)(2,1)}, u32[]{:S(2)}) copy-start(bf16[128]{0:T(256)(128)(2,1)} %param.27) | copy-start | bytes 772
  8.0 257.4 %all-reduce.14.cloned.1.call-start = ((), (), s32[]{:S(2)}) async-start(), calls=%async_computation.14 | async-start | bytes 1048576 | tf_op jit(solution)/shard_map/psum | solution.py:92
  8.1 175.9 %copy-start = (bf16[2,1280,1024]{2,1,0:T(8,128)(2,1)S(1)}, bf16[2,1280,1024]{2,1,0:T(8,128)(2,1)}, u32[]{:S(2)}) copy-start(bf16[2,1280,1024]{2,1,0:T(8,128)(2,1)} %param.16) | copy-start | bytes 15728644
  9.4 177.5 %copy-start.82 = (f32[64]{0:T(128)}, f32[64]{0:T(128)S(1)}, u32[]{:S(2)}) copy-start(f32[64]{0:T(128)S(1)} %get-tuple-element.104) | copy-start | bytes 772
  9.4 177.5 %copy-start.84 = (f32[64]{0:T(128)}, f32[64]{0:T(128)S(1)}, u32[]{:S(2)}) copy-start(f32[64]{0:T(128)S(1)} %get-tuple-element.105) | copy-start | bytes 772
  10.9 176.0 %copy-start.113 = (f32[64]{0:T(128)}, f32[64]{0:T(128)S(1)}, u32[]{:S(2)}) copy-start(f32[64]{0:T(128)S(1)} %get-tuple-element.42) | copy-start | bytes 772
  10.9 176.0 %copy-start.115 = (f32[64]{0:T(128)}, f32[64]{0:T(128)S(1)}, u32[]{:S(2)}) copy-start(f32[64]{0:T(128)S(1)} %get-tuple-element.41) | copy-start | bytes 772
  11.0 176.0 %copy-start.102 = (f32[64]{0:T(128)}, f32[64]{0:T(128)S(1)}, u32[]{:S(2)}) copy-start(f32[64]{0:T(128)S(1)} %fusion.136) | copy-start | bytes 772
  11.0 138.6 %copy-start.100 = (f32[64]{0:T(128)}, f32[64]{0:T(128)S(1)}, u32[]{:S(2)}) copy-start(f32[64]{0:T(128)S(1)} %fusion.138) | copy-start | bytes 772
  33.3 113.2 %copy-start.54 = (f32[8,1,128]{2,1,0:T(1,128)}, f32[8,1,128]{2,1,0:T(1,128)S(1)}, u32[]{:S(2)}) copy-start(f32[8,1,128]{2,1,0:T(1,128)S(1)} %convert_element_type.418) | copy-start | bytes 12292
  228.3 49.0 %all-gather.9.cloned.1.call-start = ((), (), s32[]{:S(2)}) async-start(), calls=%async_computation.6 | async-start | bytes 2359296 | tf_op jit(solution)/shard_map/all_gather | solution.py:243
  228.9 99.4 %all-gather.11.cloned.1.call-start = ((), (), s32[]{:S(2)}) async-start(), calls=%async_computation.7 | async-start | bytes 2359296 | tf_op jit(solution)/shard_map/all_gather | solution.py:244
  229.5 138.2 %all-reduce.18.cloned.1.call-start = ((), (), s32[]{:S(2)}) async-start(), calls=%async_computation.16 | async-start | bytes 524288 | tf_op jit(solution)/shard_map/psum | solution.py:126
  337.3 165.8 %all-reduce.16.cloned.1.call-start = ((), (), s32[]{:S(2)}) async-start(), calls=%async_computation.15 | async-start | bytes 11534336 | tf_op jit(solution)/shard_map/psum | solution.py:108
  391.0 194.9 %reduce-scatter.11.cloned.1.call-start = ((), (), s32[]{:S(2)}) async-start(), calls=%async_computation.10 | async-start | bytes 589824 | tf_op jit(solution)/shard_map/reduce_scatter | solution.py:264
  397.3 188.6 %reduce-scatter.9.cloned.1.call-start = ((), (), s32[]{:S(2)}) async-start(), calls=%async_computation.9 | async-start | bytes 589824 | tf_op jit(solution)/shard_map/reduce_scatter | solution.py:263
  398.0 192.4 %reduce-scatter.13.cloned.1.call-start = ((), (), s32[]{:S(2)}) async-start(), calls=%async_computation.11 | async-start | bytes 589824 | tf_op jit(solution)/shard_map/reduce_scatter | solution.py:265
  399.3 256.0 %reduce-scatter.7.cloned.1.call-start = ((), (), s32[]{:S(2)}) async-start(), calls=%async_computation.8 | async-start | bytes 589824 | tf_op jit(solution)/shard_map/reduce_scatter | solution.py:262
  400.9 345.7 %reduce-scatter.15.cloned.1.call-start = ((), (), s32[]{:S(2)}) async-start(), calls=%async_computation.12 | async-start | bytes 4718592 | tf_op jit(solution)/shard_map/reduce_scatter | solution.py:266
  404.8 434.1 %reduce-scatter.17.cloned.1.call-start = ((), (), s32[]{:S(2)}) async-start(), calls=%async_computation.13 | async-start | bytes 4718592 | tf_op jit(solution)/shard_map/reduce_scatter | solution.py:267
  406.1 101.5 %copy-start.66 = (f32[8,1,128]{2,1,0:T(1,128)S(1)}, f32[8,1,128]{2,1,0:T(1,128)}, u32[]{:S(2)}) copy-start(f32[8,1,128]{2,1,0:T(1,128)} %copy-done.65) | copy-start | bytes 12292
  409.3 106.2 %slice-start = ((s8[5242880]{0:T(1024)(128)(4,1)}), s8[1048576]{0:T(1024)(128)(4,1)S(1)}, s32[]{:S(2)}) async-start(s8[5242880]{0:T(1024)(128)(4,1)} %bitcast.213), calls=%async_computation.17 | async-start | bytes 2097152
  (117 other events, 1852.7 us)
Sparse Core Ops, SparseCore 0:
  228.5 30.5 all-reduce.13
  337.4 30.2 all-reduce.17
  391.1 112.0 all-reduce.15
Sparse Core Ops, SparseCore 1:
  230.9 46.4 all-gather.8
  279.3 49.0 all-gather.10
  397.3 62.1 reduce-scatter.10
  463.4 61.0 reduce-scatter.8
  528.8 61.5 reduce-scatter.12
  594.3 60.9 reduce-scatter.6
  659.8 86.8 reduce-scatter.14
  750.7 88.0 reduce-scatter.16
where the time goes:
time: 847 us; the launch traced here: 846 us
  waiting for transfers between devices  428 us (51%)
  blocking collectives  266 us (31%)
  other arithmetic  60.1 us (7%)
  matrix products  58.8 us (7%)
  between operations  17.9 us (2%)
  local copies, waits for them, and re-layouts  14.8 us (2%)
    reduce_scatter x1, waiting for transfers between devices, local(): lax.psum_scatter(grads[5], 'dp', scatter_dimension=1, tiled=True)  92.2 us
    reduce_scatter x1, waiting for transfers between devices, local(): lax.psum_scatter(grads[4], 'dp', scatter_dimension=0, tiled=True)  91.4 us
    psum x1, waiting for transfers between devices, micro_step(): lax.psum(jnp.einsum('pye,ej->pyj', active_units, down_projection_weight,...  91.3 us
    reduce_scatter x1, waiting for transfers between devices, local(): lax.psum_scatter(grads[0], 'dp', scatter_dimension=0, tiled=True)  64.9 us
    all_gather x1, waiting for transfers between devices, local(): lax.all_gather(down_projection_weight, 'dp', axis=1, tiled=True)  47.8 us
    unnamed x1, blocking collectives  38.6 us
    all_gather x1, blocking collectives, local(): lax.all_gather(query_matrix, 'dp', axis=0, tiled=True)  31 us
    all_gather x1, blocking collectives, local(): lax.all_gather(v_weight, 'dp', axis=0, tiled=True)  31 us
  transfers between devices with their start and end apart: 11, of which 8 were waited for; matrix products, arithmetic and copies ran while one was open for 9% of the time, Pallas kernels for 0%

commit v1 on v0

--- a/solution.py
+++ b/solution.py
@@ -1,10 +1,793 @@
+import functools
+
 import jax
 import jax.numpy as jnp
 from jax import lax
+from jax.experimental import pallas as pl
+from jax.experimental.pallas import tpu as pltpu
 from jax.sharding import PartitionSpec as P
 
 HEAD = 64
 PATCH = 256
+EPS = 1e-05
+F32 = jnp.float32
+BF16 = jnp.bfloat16
+MESH = pl.DeviceIdType.MESH
+NN = (((1,), (0,)), ((), ()))
+NT = (((1,), (1,)), ((), ()))
+TN = (((0,), (0,)), ((), ()))
+SEMS = 160
+
+
+def dot(a, b, dims):
+    return lax.dot_general(a, b, dims, preferred_element_type=F32)
+
+
+def at(start, size):
+    return pl.ds(pl.multiple_of(start, size), size)
+
+
+class Wire:
+    def __init__(self, send_sem, recv_sem):
+        self.send_sem, self.recv_sem = send_sem, recv_sem
+        self.used, self.sent = 0, []
+
+    def take(self, count=1):
+        first = self.used
+        self.used += count
+        assert self.used <= SEMS
+        return first
+
+    def make(self, slot, src, dst, dev):
+        return pltpu.make_async_remote_copy(
+            src_ref=src,
+            dst_ref=dst,
+            send_sem=self.send_sem.at[slot],
+            recv_sem=self.recv_sem.at[slot],
+            device_id=dev,
+            device_id_type=MESH,
+        )
+
+    def send(self, src, dst, dev):
+        copy = self.make(self.take(), src, dst, dev)
+        copy.start()
+        self.sent.append(copy)
+        return copy
+
+    def drain(self):
+        for copy in self.sent:
+            copy.wait_send()
+
+
+def norm_back(z, mean, rstd, gain, dy):
+    zhat = (z - mean) * rstd
+    t = dy * gain
+    mt = jnp.mean(t, axis=-1, keepdims=True)
+    mz = jnp.mean(t * zhat, axis=-1, keepdims=True)
+    return rstd * (t - mt - zhat * mz), zhat
+
+
+def layer_kernel(
+    counts,
+    media,
+    latents,
+    cot,
+    wq,
+    wk,
+    wv,
+    wo,
+    up,
+    down,
+    mg,
+    mb,
+    lg,
+    lb,
+    fg,
+    fb,
+    lat_out,
+    media_out,
+    lgrad_out,
+    gq,
+    gk,
+    gv,
+    go,
+    gup,
+    gdown,
+    vec0,
+    vec1,
+    vec2,
+    vec3,
+    vec4,
+    vec5,
+    send_sem,
+    recv_sem,
+    local_sem,
+    prm_own,
+    prm,
+    vec,
+    xin,
+    lat,
+    kin,
+    mu,
+    rs,
+    w3,
+    wob,
+    upb,
+    dnb,
+    kb,
+    vb,
+    qb,
+    att,
+    attl,
+    mix,
+    mid,
+    hid,
+    cota,
+    act,
+    ig,
+    hgs,
+    hgr,
+    hgx,
+    fos,
+    fors,
+    fox,
+    gus,
+    gur,
+    guo,
+    gu,
+    gua,
+    gds,
+    gdr,
+    gdo,
+    gd,
+    gda,
+    midg,
+    lowb,
+    mgr,
+    kvg,
+    qg,
+    cgs,
+    cgr,
+    gown,
+    g1,
+    yr,
+    g2,
+    zr,
+    dxs,
+    accg,
+    accb,
+    mgo,
+    outl,
+    outg,
+    vgs,
+    vgc,
+    vgt,
+    vga,
+):
+    i = lax.axis_index("dp")
+    j = lax.axis_index("mp")
+    x, c = j // 2, j % 2
+    yy, z = i % 2, i // 2
+    zlo, zhi = z % 2, z // 2
+    r = i % 4
+
+    def peer(k):
+        a = 1 - yy if k & 1 else yy
+        b = 1 - zlo if k & 2 else zlo
+        d = 1 - zhi if k & 4 else zhi
+        return d * 4 + b * 2 + a
+
+    jx = j + 2 - 4 * x
+    jc = j + 1 - 2 * c
+    ox = 1 - x
+    oc = 1 - c
+    xpart = (i, jx)
+    cpart = (i, jc)
+    ypart = (peer(1), j)
+    wire = Wire(send_sem, recv_sem)
+
+    def w3b(ii, xx, cc):
+        return w3.at[xx, ii, :, at(cc * 384, 128 * 3)]
+
+    local = []
+
+    def bring(src, dst):
+        copy = pltpu.make_async_copy(src, dst, local_sem.at[len(local)])
+        copy.start()
+        local.append(copy)
+        return copy
+
+    bring(wk, w3.at[x, i, :, at(c * 384, 128)])
+    bring(wv, w3.at[x, i, :, at(c * 384 + 128, 128)])
+    bring(wq, w3.at[x, i, :, at(c * 384 + 256, 128)])
+    bring(wo, wob.at[j, :, at(i * 128, 128)])
+    in_lat = bring(latents.at[c], lat)
+    in_media = bring(media.at[c], xin)
+    in_cot = bring(cot.at[c], cota.at[r])
+    in_up = bring(up.at[:, at(r * 256, 256)], upb.at[i, :, at(c * 256, 256)])
+    in_dn = bring(down.at[at(r * 256, 256), :], dnb.at[c, :, at(i * 128, 128)])
+    for row, ref in enumerate((mg, mb, lg, lb, fg, fb)):
+        prm_own[row : row + 1, :] = ref[...].astype(F32)
+    prm_own[6:8, :] = jnp.zeros((2, 128), F32)
+    prm[i] = prm_own[...]
+
+    barrier = pltpu.get_barrier_semaphore()
+    partners = [(peer(k), j) for k in range(1, 8)] + [xpart, cpart]
+    partners += [(peer(k), jx) for k in range(1, 4)]
+    for dev in partners:
+        pl.semaphore_signal(barrier, inc=1, device_id=dev, device_id_type=MESH)
+    pl.semaphore_wait(barrier, len(partners))
+
+    got_prm = [wire.send(prm_own, prm.at[i], (peer(k), j)) for k in range(1, 8)]
+    for copy in local[:4]:
+        copy.wait()
+
+    def wo_at(ii, jj):
+        return wob.at[jj, :, at(ii * 128, 128)]
+
+    def same(view, dev):
+        return wire.send(view, view, dev)
+
+    z3 = [same(w3b(i, x, c), (peer(2 * k), j)) for k in (1, 2, 3)]
+    y3 = [same(w3b(i, x, c), ypart)]
+    x3 = [same(w3b(i, x, c), xpart)]
+    zo = [same(wo_at(i, j), (peer(2 * k), j)) for k in (1, 2, 3)]
+    yo = [same(wo_at(i, j), ypart)]
+    xo = [same(wo_at(i, j), xpart)]
+
+    for copy in got_prm:
+        copy.wait_recv()
+    for ii in range(8):
+        vec[:, ii * 128 : (ii + 1) * 128] = prm[ii]
+
+    in_lat.wait()
+    lat32 = lat[...].astype(F32)
+    lmean = jnp.mean(lat32, axis=-1, keepdims=True)
+    lcen = lat32 - lmean
+    lrs = lax.rsqrt(jnp.mean(lcen * lcen, axis=-1, keepdims=True) + EPS)
+    kin[1280:1344, :] = (lcen * lrs * vec[2:3, :] + vec[3:4, :]).astype(BF16)
+    mu[1280:1344, :] = lmean
+    rs[1280:1344, :] = lrs
+    in_media.wait()
+
+    def media_norm(lo, hi):
+        def strip(t, carry):
+            rows = at(t * 16, 16)
+            v = xin[rows, :].astype(F32)
+            m = jnp.mean(v, axis=-1, keepdims=True)
+            cen = v - m
+            rr = lax.rsqrt(jnp.mean(cen * cen, axis=-1, keepdims=True) + EPS)
+            kin[rows, :] = (cen * rr * vec[0:1, :] + vec[1:2, :]).astype(BF16)
+            mu[rows, :] = m
+            rs[rows, :] = rr
+            return carry
+
+        lax.fori_loop(lo, hi, strip, 0)
+
+    media_norm(0, 40)
+    for k in (1, 2, 3):
+        z3[k - 1].wait_recv()
+        y3.append(same(w3b(peer(2 * k), x, c), ypart))
+        x3.append(same(w3b(peer(2 * k), x, c), xpart))
+    in_cot.wait()
+    cots = [wire.send(cota.at[r], cota.at[r], (peer(k), j)) for k in (1, 2, 3)]
+    ups, dns = [], []
+    for k in range(1, 8):
+        rk = peer(k) % 4
+        ups.append(
+            wire.send(
+                up.at[:, at(rk * 256, 256)], upb.at[i, :, at(c * 256, 256)], (peer(k), j)
+            )
+        )
+    for k in range(1, 8):
+        rk = peer(k) % 4
+        dns.append(
+            wire.send(
+                down.at[at(rk * 256, 256), :], dnb.at[c, :, at(i * 128, 128)], (peer(k), j)
+            )
+        )
+    media_norm(40, 60)
+    for k in (0, 1, 2, 3):
+        y3[k].wait_recv()
+        x3.append(same(w3b(peer(2 * k + 1), x, c), xpart))
+    own3 = w3.at[x, :, :, at(c * 384, 128 * 3)]
+    c3 = same(own3, cpart)
+    for k in (1, 2, 3):
+        zo[k - 1].wait_recv()
+        yo.append(same(wo_at(peer(2 * k), j), ypart))
+        xo.append(same(wo_at(peer(2 * k), j), xpart))
+    media_norm(60, 80)
+    for k in (0, 1, 2, 3):
+        yo[k].wait_recv()
+        xo.append(same(wo_at(peer(2 * k + 1), j), xpart))
+    co = same(wob.at[j], cpart)
+    c3.wait_recv()
+
+    count = counts[c]
+    head_of_lane = lax.broadcasted_iota(jnp.int32, (256, 256), 1) // HEAD
+    head_of_row = lax.broadcasted_iota(jnp.int32, (256, 256), 0) // HEAD
+    own_head = head_of_lane == head_of_row
+    lane64 = lax.broadcasted_iota(jnp.int32, (64, 256), 1) // HEAD
+
+    def spread(v):
+        v = v.astype(F32)
+        return jnp.where(own_head, jnp.concatenate([v, v, v, v], axis=0), 0.0).astype(BF16)
+
+    def gather_heads(v):
+        out = jnp.zeros((64, 256), F32)
+        for h in range(4):
+            out = jnp.where(lane64 == h, v[h * 64 : (h + 1) * 64, :], out)
+        return out
+
+    def w_kv(g, cc):
+        return w3[g, :, :, cc * 384 : cc * 384 + 256].reshape(1024, 256)
+
+    def w_q(g, cc):
+        return w3[g, :, :, cc * 384 + 256 : cc * 384 + 384].reshape(1024, 128)
+
+    def attention(g):
+        def project(t, carry):
+            rows = at(t * 448, 448)
+            a = kin[rows, :]
+            for cc in (0, 1):
+                o = dot(a, w_kv(g, cc), NN)
+                kb[g, rows, cc * 128 : (cc + 1) * 128] = o[:, :128].astype(BF16)
+                vb[g, rows, cc * 128 : (cc + 1) * 128] = o[:, 128:].astype(BF16)
+            return carry
+
+        lax.fori_loop(0, 3, project, 0)
+        for cc in (0, 1):
+            qb[g, :, cc * 128 : (cc + 1) * 128] = dot(
+                kin[1280:1344, :], w_q(g, cc), NN
+            ).astype(BF16)
+        q4 = spread(qb[g])
+
+        def score(t, top):
+            rows = at(t * 192, 192)
+            s = dot(kb[g, rows, :], q4, NT) * 0.125
+            key = lax.broadcasted_iota(jnp.int32, (192, 256), 0) + t * 192
+            ok = jnp.logical_or(key < count * PATCH, key >= 1280)
+            s = jnp.where(ok, s, -1e30)
+            att[g, rows, :] = s
+            return jnp.maximum(top, jnp.max(s, axis=0, keepdims=True))
+
+        top = lax.fori_loop(0, 7, score, jnp.full((1, 256), -1e30, F32))
+
+        def raise_(t, total):
+            rows = at(t * 64, 64)
+            e = jnp.exp(att[g, rows, :] - top)
+            att[g, rows, :] = e
+            return total + jnp.sum(e, axis=0, keepdims=True)
+
+        total = lax.fori_loop(0, 21, raise_, jnp.zeros((1, 256), F32))
+        scale = 1.0 / total
+
+        def level(t, carry):
+            rows = at(t * 64, 64)
+            p = att[g, rows, :] * scale
+            att[g, rows, :] = p
+            attl[g, rows, :] = p.astype(BF16)
+            return carry
+
+        lax.fori_loop(0, 21, level, 0)
+        mixed = dot(attl[g], vb[g], TN)
+        mix[:, at(g * 256, 256)] = gather_heads(mixed).astype(BF16)
+
+    attention(x)
+    for copy in x3:
+        copy.wait_recv()
+    oth3 = w3.at[ox, :, :, at(c * 384, 128 * 3)]
+    c3b = same(oth3, cpart)
+    for copy in xo:
+        copy.wait_recv()
+    cob = same(wob.at[jx], cpart)
+    c3b.wait_recv()
+    attention(ox)
+    co.wait_recv()
+    cob.wait_recv()
+
+    wo_all = wob[...].reshape(512, 1024)
+    middle = lat[...].astype(F32) + dot(mix[...], wo_all, NN)
+    mid[...] = middle
+    fmean = jnp.mean(middle, axis=-1, keepdims=True)
+    fcen = middle - fmean
+    frs = lax.rsqrt(jnp.mean(fcen * fcen, axis=-1, keepdims=True) + EPS)
+    hid[r] = (fcen * frs * vec[4:5, :] + vec[5:6, :]).astype(BF16)
+    hids = [wire.send(hid.at[r], hid.at[r], (peer(k), j)) for k in (3, 2, 1)]
+
+    in_up.wait()
+    in_dn.wait()
+    for copy in ups:
+        copy.wait_recv()
+    cup = same(upb.at[:, :, at(c * 256, 256)], cpart)
+    for copy in dns:
+        copy.wait_recv()
+    cdn = same(dnb.at[c], cpart)
+    for copy in hids:
+        copy.wait_recv()
+    for copy in cots:
+        copy.wait_recv()
+    cup.wait_recv()
+    cdn.wait_recv()
+
+    hid_all = hid[...].reshape(256, 1024)
+    cot_all = cota[...].reshape(256, 1024)
+    up_all = upb[...].reshape(1024, 512)
+    dn_all = dnb[...].reshape(512, 1024)
+    inner = dot(hid_all, up_all, NN)
+    phi = 0.5 * (1.0 + lax.erf(inner * (0.5**0.5)))
+    act[...] = (inner * phi).astype(BF16)
+    agrad = dot(cot_all, dn_all, NT)
+    dens = jnp.exp(inner * inner * -0.5) * 0.3989422804014327
+    ig[...] = (agrad * (phi + inner * dens)).astype(BF16)
+    hgs[...] = dot(ig[...], up_all, NT).astype(BF16).reshape(4, 64, 1024)
+
+    def reduce_sends(src, dst):
+        out = []
+        slot = x * 4 + r
+        for k in (7, 6, 5, 3, 2, 1, 4):
+            kx, kr = k // 4, k % 4
+            tx = ox if kx else x
+            tr = peer(kr) % 4
+            dev = (peer(kr), jx if kx else j)
+            out.append(wire.send(src.at[tr, at(tx * 32, 32), :], dst.at[slot], dev))
+        keep = pltpu.make_async_copy(
+            src.at[r, at(x * 32, 32), :], dst.at[slot], local_sem.at[len(local)]
+        )
+        keep.start()
+        local.append(keep)
+        return out, keep
+
+    hg_in, hg_keep = reduce_sends(hgs, hgr)
+
+    gus[...] = dot(hid_all, ig[:, at(oc * 256, 256)], TN).astype(BF16).reshape(8, 128, 256)
+    gu_in = wire.send(gus, gur, cpart)
+    gds[...] = dot(act[:, at(oc * 256, 256)], cot_all, TN).astype(BF16)
+    gd_in = wire.send(gds, gdr, cpart)
+    guo[...] = dot(hid_all, ig[:, at(c * 256, 256)], TN).reshape(8, 128, 256)
+    gdo[...] = dot(act[:, at(c * 256, 256)], cot_all, TN)
+
+    hg_keep.wait()
+    for copy in hg_in:
+        copy.wait_recv()
+
+    def sum_of(ref, n):
+        total = ref[0].astype(F32)
+        for s in range(1, n):
+            total = total + ref[s].astype(F32)
+        return total
+
+    hgx[x] = sum_of(hgr, 8).astype(BF16)
+    hgx_in = same(hgx.at[x], xpart)
+
+    fos[...] = dot(act[...], dn_all, NN).astype(BF16).reshape(4, 64, 1024)
+    gu_in.wait_recv()
+    gu[...] = (guo[...] + gur[...].astype(F32)).astype(BF16)
+    gua[i] = gu[i]
+    gu_out = [wire.send(gu.at[peer(k)], gua.at[i], (peer(k), j)) for k in (4, 5, 6, 7, 1, 2, 3)]
+    gd_in.wait_recv()
+    gd[...] = (gdo[...] + gdr[...].astype(F32)).astype(BF16)
+    gda[i] = gd[:, at(i * 128, 128)]
+    gd_out = [
+        wire.send(gd.at[:, at(peer(k) * 128, 128)], gda.at[i], (peer(k), j))
+        for k in (4, 5, 6, 7, 1, 2, 3)
+    ]
+
+    hgx_in.wait_recv()
+    fo_in, fo_keep = reduce_sends(fos, fors)
+    dy = hgx[...].reshape(64, 1024).astype(F32)
+    middle = mid[...]
+    fmean = jnp.mean(middle, axis=-1, keepdims=True)
+    fcen = middle - fmean
+    frs = lax.rsqrt(jnp.mean(fcen * fcen, axis=-1, keepdims=True) + EPS)
+    dz, zhat = norm_back(middle, fmean, frs, vec[4:5, :], dy)
+
+    def put_vec(k, v):
+        for ii in range(8):
+            vgs[ii, k : k + 1, :] = v[:, ii * 128 : (ii + 1) * 128]
+
+    put_vec(4, jnp.sum(dy * zhat, axis=0, keepdims=True))
+    put_vec(5, jnp.sum(dy, axis=0, keepdims=True))
+    middle_grad = cota[r].astype(F32) + dz
+    midg[...] = middle_grad
+    low = middle_grad.astype(BF16)
+    wo_all = wob[...].reshape(512, 1024)
+    mgr_all = dot(low, wo_all, NT).astype(BF16)
+    for g in (0, 1):
+        mgr[g] = mgr_all[:, g * 256 : (g + 1) * 256]
+    lowb[...] = low
+
+    def back(g):
+        m4 = spread(mgr[g])
+        q4 = spread(qb[g])
+
+        def first(t, delta):
+            rows = at(t * 192, 192)
+            vg = dot(attl[g, rows, :], m4, NN).astype(BF16)
+            kvg[rows, at(g * 512 + 128, 128)] = vg[:, :128]
+            kvg[rows, at(g * 512 + 384, 128)] = vg[:, 128:]
+            ag = dot(vb[g, rows, :], m4, NT)
+            pa = att[g, rows, :] * ag
+            dxs[rows, 0:256] = pa
+            return delta + jnp.sum(pa, axis=0, keepdims=True)
+
+        delta = lax.fori_loop(0, 7, first, jnp.zeros((1, 256), F32))
+
+        def second(t, total):
+            rows = at(t * 192, 192)
+            sg = (dxs[rows, 0:256] - att[g, rows, :] * delta).astype(BF16)
+            kg = (dot(sg, q4, NN) * 0.125).astype(BF16)
+            kvg[rows, at(g * 512, 128)] = kg[:, :128]
+            kvg[rows, at(g * 512 + 256, 128)] = kg[:, 128:]
+            return total + dot(sg, kb[g, rows, :], TN)
+
+        total = lax.fori_loop(0, 7, second, jnp.zeros((256, 256), F32))
+        qg[g] = (gather_heads(total) * 0.125).astype(BF16)
+
+    back(x)
+    def weight_tile(t, carry):
+        cols = at(t * 256, 256)
+        two = pl.ds(t * 2, 2)
+        o = dot(kin[:, cols], kvg[:, at(x * 512 + oc * 256, 256)], TN)
+        cgs[two, :, 0:256] = o.astype(BF16).reshape(2, 128, 256)
+        gown[cols, 0:256] = dot(kin[:, cols], kvg[:, at(x * 512 + c * 256, 256)], TN)
+        return carry
+
+    lax.fori_loop(0, 4, weight_tile, 0)
+
+    def small_tile(t, carry):
+        cols = at(t * 256, 256)
+        dxs[cols, 0:256] = dot(kin[1280:1344, cols], qg[x], TN)
+        dxs[cols, 256:512] = dot(lowb[:, cols], mix[:, at(x * 256, 256)], TN)
+        return carry
+
+    lax.fori_loop(0, 4, small_tile, 0)
+    gown[:, 256:384] = dxs[0:1024, at(c * 128, 128)]
+    gown[:, 384:512] = dxs[0:1024, at(256 + c * 128, 128)]
+    cgs[:, :, 256:384] = dxs[0:1024, at(oc * 128, 128)].astype(BF16).reshape(8, 128, 128)
+    cgs[:, :, 384:512] = dxs[0:1024, at(256 + oc * 128, 128)].astype(BF16).reshape(8, 128, 128)
+    cg_in = wire.send(cgs, cgr, cpart)
+
+    back(ox)
+
+    cg_in.wait_recv()
+    g1[...] = (
+        (gown[...].reshape(8, 128, 512) + cgr[...].astype(F32)).astype(BF16).reshape(4, 2, 128, 512)
+    )
+    y_in = wire.send(g1.at[:, 1 - yy], yr, ypart)
+
+    def dx_tile(rows):
+        w_all = jnp.concatenate([w_kv(0, 0), w_kv(0, 1), w_kv(1, 0), w_kv(1, 1)], axis=1)
+        return dot(kvg[rows, :], w_all, NT)
+
+    accg[...] = jnp.zeros((8, 1024), F32)
+    accb[...] = jnp.zeros((8, 1024), F32)
+    out_base = wire.take(5)
+
+    def out_copy(t, slot):
+        rows = at(t * 256, 256)
+        return wire.make(slot, mgo.at[rows, :], media_out.at[c, rows, :], cpart)
+
+    def keep_copy(t):
+        rows = at(t * 256, 256)
+        return pltpu.make_async_copy(
+            mgo.at[rows, :], media_out.at[c, rows, :], local_sem.at[20 + t]
+        )
+
+    def media_back(t, carry):
+        dxs[0:256, :] = dx_tile(at(t * 256, 256))
+
+        def strip(u, carry):
+            here = at(u * 16, 16)
+            rows = at(t * 256 + u * 16, 16)
+            v = xin[rows, :].astype(F32)
+            dy = dxs[here, :]
+            dz, zhat = norm_back(v, mu[rows, :], rs[rows, :], vec[0:1, :], dy)
+            mgo[rows, :] = dz.astype(BF16)
+            pz = dy * zhat
+            accg[...] += pz[0:8, :] + pz[8:16, :]
+            accb[...] += dy[0:8, :] + dy[8:16, :]
+            return carry
+
+        lax.fori_loop(0, 16, strip, 0)
+        out_copy(t, out_base + t).start()
+        keep_copy(t).start()
+        return carry
+
+    lax.fori_loop(0, 5, media_back, 0)
+    put_vec(0, jnp.sum(accg[...], axis=0, keepdims=True))
+    put_vec(1, jnp.sum(accb[...], axis=0, keepdims=True))
+    dxs[0:64, :] = dx_tile(pl.ds(1280, 64))
+    q_all = jnp.concatenate([qg[0], qg[1]], axis=1)
+    wq_all = jnp.concatenate([w_q(0, 0), w_q(0, 1), w_q(1, 0), w_q(1, 1)], axis=1)
+    lsum = dxs[0:64, :] + dot(q_all, wq_all, NT)
+    lat32 = lat[...].astype(F32)
+    dz, zhat = norm_back(lat32, mu[1280:1344, :], rs[1280:1344, :], vec[2:3, :], lsum)
+    outg[...] = (midg[...] + dz).astype(BF16)
+    lg_in = wire.send(outg, lgrad_out.at[c], cpart)
+    lg_keep = pltpu.make_async_copy(outg, lgrad_out.at[c], local_sem.at[25])
+    lg_keep.start()
+    put_vec(2, jnp.sum(lsum * zhat, axis=0, keepdims=True))
+    put_vec(3, jnp.sum(lsum, axis=0, keepdims=True))
+    for ii in range(8):
+        vgs[ii, 6:8, :] = jnp.zeros((2, 128), F32)
+    vg_in = wire.send(vgs, vgc, cpart)
+
+    y_in.wait_recv()
+    total = g1[:, yy].astype(F32) + yr[...].astype(F32)
+    g2[...] = total.astype(BF16)
+    z_in = [wire.send(g2.at[peer(2 * k) // 2], zr.at[z], (peer(2 * k), j)) for k in (1, 2, 3)]
+    zr[z] = g2[z]
+
+    vg_in.wait_recv()
+    vgt[...] = vgs[...] + vgc[...]
+    vga[i] = vgt[i]
+    v_in = [wire.send(vgt.at[peer(k)], vga.at[i], (peer(k), j)) for k in range(1, 8)]
+
+    fo_keep.wait()
+    for copy in fo_in:
+        copy.wait_recv()
+    fox[x] = sum_of(fors, 8).astype(BF16)
+    fox_in = same(fox.at[x], xpart)
+
+    for copy in gu_out:
+        copy.wait_recv()
+    for q in range(4):
+        gup[:, q * 256 : (q + 1) * 256] = gua[q].astype(F32) + gua[4 + q].astype(F32)
+    for copy in gd_out:
+        copy.wait_recv()
+    for q in range(4):
+        gdown[q * 256 : (q + 1) * 256, :] = gda[q].astype(F32) + gda[4 + q].astype(F32)
+
+    fox_in.wait_recv()
+    outl[...] = (mid[...] + fox[...].reshape(64, 1024).astype(F32)).astype(BF16)
+    lo_in = wire.send(outl, lat_out.at[c], cpart)
+    lo_keep = pltpu.make_async_copy(outl, lat_out.at[c], local_sem.at[26])
+    lo_keep.start()
+
+    for copy in z_in:
+        copy.wait_recv()
+    last = sum_of(zr, 4)
+    gk[...] = last[:, 0:128]
+    gv[...] = last[:, 128:256]
+    gq[...] = last[:, 256:384]
+    go[...] = last[:, 384:512].T
+    for copy in v_in:
+        copy.wait_recv()
+    sums = sum_of(vga, 8)
+    for k, ref in enumerate((vec0, vec1, vec2, vec3, vec4, vec5)):
+        ref[...] = sums[k : k + 1, :]
+
+    for t in range(5):
+        keep_copy(t).wait()
+        out = out_copy(t, out_base + t)
+        out.wait_send()
+        out.wait_recv()
+    lg_keep.wait()
+    lo_keep.wait()
+    lg_in.wait_recv()
+    lo_in.wait_recv()
+    wire.drain()
+
+
+SCRATCH = (
+    ("prm_own", (8, 128), F32),
+    ("prm", (8, 8, 128), F32),
+    ("vec", (8, 1024), F32),
+    ("xin", (1280, 1024), BF16),
+    ("lat", (64, 1024), BF16),
+    ("kin", (1344, 1024), BF16),
+    ("mu", (1344, 1), F32),
+    ("rs", (1344, 1), F32),
+    ("w3", (2, 8, 128, 768), BF16),
+    ("wob", (4, 128, 1024), BF16),
+    ("upb", (8, 128, 512), BF16),
+    ("dnb", (2, 256, 1024), BF16),
+    ("kb", (2, 1344, 256), BF16),
+    ("vb", (2, 1344, 256), BF16),
+    ("qb", (2, 64, 256), BF16),
+    ("att", (2, 1344, 256), F32),
+    ("attl", (2, 1344, 256), BF16),
+    ("mix", (64, 512), BF16),
+    ("mid", (64, 1024), F32),
+    ("hid", (4, 64, 1024), BF16),
+    ("cota", (4, 64, 1024), BF16),
+    ("act", (256, 512), BF16),
+    ("ig", (256, 512), BF16),
+    ("hgs", (4, 64, 1024), BF16),
+    ("hgr", (8, 32, 1024), BF16),
+    ("hgx", (2, 32, 1024), BF16),
+    ("fos", (4, 64, 1024), BF16),
+    ("fors", (8, 32, 1024), BF16),
+    ("fox", (2, 32, 1024), BF16),
+    ("gus", (8, 128, 256), BF16),
+    ("gur", (8, 128, 256), BF16),
+    ("guo", (8, 128, 256), F32),
+    ("gu", (8, 128, 256), BF16),
+    ("gua", (8, 128, 256), BF16),
+    ("gds", (256, 1024), BF16),
+    ("gdr", (256, 1024), BF16),
+    ("gdo", (256, 1024), F32),
+    ("gd", (256, 1024), BF16),
+    ("gda", (8, 256, 128), BF16),
+    ("midg", (64, 1024), F32),
+    ("lowb", (64, 1024), BF16),
+    ("mgr", (2, 64, 256), BF16),
+    ("kvg", (1344, 1024), BF16),
+    ("qg", (2, 64, 256), BF16),
+    ("cgs", (8, 128, 512), BF16),
+    ("cgr", (8, 128, 512), BF16),
+    ("gown", (1024, 512), F32),
+    ("g1", (4, 2, 128, 512), BF16),
+    ("yr", (4, 128, 512), BF16),
+    ("g2", (4, 128, 512), BF16),
+    ("zr", (4, 128, 512), BF16),
+    ("dxs", (1344, 1024), F32),
+    ("accg", (8, 1024), F32),
+    ("accb", (8, 1024), F32),
+    ("mgo", (1280, 1024), BF16),
+    ("outl", (64, 1024), BF16),
+    ("outg", (64, 1024), BF16),
+    ("vgs", (8, 8, 128), F32),
+    ("vgc", (8, 8, 128), F32),
+    ("vgt", (8, 8, 128), F32),
+    ("vga", (8, 8, 128), F32),
+)
+
+
+def fused(media, latents, cotangent, image_counts, wq, wk, wv, wo, up, down, *gains):
+    anyspace = pl.BlockSpec(memory_space=pl.ANY)
+    vmem = pl.BlockSpec(memory_space=pltpu.VMEM)
+    smem = pl.BlockSpec(memory_space=pltpu.SMEM)
+    shape = jax.ShapeDtypeStruct
+    outs = pl.pallas_call(
+        layer_kernel,
+        out_shape=[
+            shape(latents.shape, BF16),
+            shape(media.shape, BF16),
+            shape(latents.shape, BF16),
+            shape(wq.shape, F32),
+            shape(wk.shape, F32),
+            shape(wv.shape, F32),
+            shape(wo.shape, F32),
+            shape(up.shape, F32),
+            shape(down.shape, F32),
+        ]
+        + [shape((1, 128), F32)] * 6,
+        in_specs=[smem] + [anyspace] * 9 + [vmem] * 6,
+        out_specs=[anyspace] * 3 + [vmem] * 12,
+        scratch_shapes=[
+            pltpu.SemaphoreType.DMA((SEMS,)),
+            pltpu.SemaphoreType.DMA((SEMS,)),
+            pltpu.SemaphoreType.DMA((32,)),
+        ]
+        + [pltpu.VMEM(size, kind) for _, size, kind in SCRATCH],
+        compiler_params=pltpu.CompilerParams(
+            collective_id=0, has_side_effects=True, vmem_limit_bytes=60 * 2**20
+        ),
+        cost_estimate=pl.CostEstimate(
+            flops=14 * 10**9, bytes_accessed=20 * 10**6, transcendentals=10**6
+        ),
+    )(
+        image_counts,
+        media,
+        latents,
+        cotangent,
+        wq,
+        wk,
+        wv,
+        wo,
+        up,
+        down,
+        *[v.reshape(1, 128) for v in gains],
+    )
+    return tuple(outs[:9]) + tuple(v.reshape(128) for v in outs[9:])
+
+
+def fits(mesh):
+    return mesh.shape["dp"] == 8 and mesh.shape["mp"] == 4
+
+
 MB = 2
 SB = 1
 
@@ -315,7 +1098,7 @@
         P("dp"),
     )
     return jax.shard_map(
-        local,
+        fused if fits(mesh) else local,
         mesh=mesh,
         in_specs=placed,
         out_specs=(

time: 847 us -> 142 us (0.17)
  waiting for transfers between devices: 428 us -> 0 us
  blocking collectives: 266 us -> 0 us
  Pallas kernels: 0 us -> 126 us
  other arithmetic: 60.1 us -> 0 us
  matrix products: 58.8 us -> 0 us
  between operations: 17.9 us -> 0.75 us
    reduce_scatter x6 -> x0, waiting for transfers between devices: 253 us -> none  [the longest x1 92.2 us: local(): lax.psum_scatter(grads[5], 'dp', scatter_dimension=1, tiled=True)]
    all_gather x10 -> x0, blocking collectives: 227 us -> none  [the longest x1 31 us: local(): lax.all_gather(query_matrix, 'dp', axis=0, tiled=True)]
    pallas_call x0 -> x1, Pallas kernels: none -> 126 us  [fused(): pl.pallas_call(layer_kernel, out_shape=[shape(latents.shape, BF16), shape...]
    psum x3 -> x0, waiting for transfers between devices: 117 us -> none  [the longest x1 91.3 us: micro_step(): lax.psum(jnp.einsum('pye,ej->pyj', active_units, down_projection_weight,...]
    dot_general x48 -> x0, matrix products: 58.8 us -> none  [the longest x2 4.96 us: micro_step(): jnp.einsum('pye,ej->pyj', active_units, down_projection_weight, preferred...]
    all_gather x2 -> x0, waiting for transfers between devices: 56.6 us -> none  [the longest x1 47.8 us: local(): lax.all_gather(down_projection_weight, 'dp', axis=1, tiled=True)]
    unnamed x1 -> x0, blocking collectives: 38.6 us -> none
    reduce_sum x15 -> x0, other arithmetic: 26.8 us -> none  [the longest x5 17.8 us: layer_norm(): return center * lax.rsqrt(spread + 1e-05) * gain + bias]
  transfers between devices with their start and end apart: 11 -> 0, of which waited for: 8 -> 0; matrix products, arithmetic and copies ran while one was open for 9% -> 0% of each run, Pallas kernels for 0% -> 0%
where the time goes in v1:
time: 142 us
  Pallas kernels  126 us (89%)
  local copies, waits for them, and re-layouts  15.1 us (11%)
    pallas_call x1, Pallas kernels, fused(): pl.pallas_call(layer_kernel, out_shape=[shape(latents.shape, BF16), shape...  126 us
    unnamed x41, local copies, waits for them, and re-layouts  15.1 us

profile of v1, /device:TPU:0, one launch (start us, length us, event | category | flops | bytes accessed | tf_op | source)
XLA Modules:
  0.0 141.7 jit_solution(781136540375338611)
XLA Ops:
  0.7 125.8 %shard_map.271 = (bf16[2,64,1024]{2,1,0:T(8,128)(2,1)}, bf16[2,1280,1024]{2,1,0:T(8,128)(2,1)}, bf16[2,64,1024]{2,1,0:T(8,128)(2,1)}, f32[128,128]{1,0:T(8,128)}...) custom-call(s32[2]{0:T(128)} %counts.1, ...), custom_call_target="tpu_custom_call" | custom-call | flops 14000000000 | bytes 20000000 | tf_op jit(solution)/shard_map/pallas_call | solution.py:743
  126.5 1.7 %copy.46 = bf16[2,64,1024]{2,1,0:T(8,128)(2,1)} copy(bf16[2,64,1024]{2,1,0:T(8,128)(2,1)} %get-tuple-element.60) | data formatting | bytes 524288
  128.2 0.0 copy-start.3
  128.2 0.0 copy-start.1
  128.2 0.0 copy-start
  128.2 0.0 copy-start.12
  128.2 0.0 copy-start.11
  128.2 0.0 copy-start.10
  128.2 0.0 copy-start.9
  128.2 0.0 copy-start.8
  128.3 5.5 %copy.47 = bf16[2,1280,1024]{2,1,0:T(8,128)(2,1)} copy(bf16[2,1280,1024]{2,1,0:T(8,128)(2,1)} %get-tuple-element.61) | data formatting | bytes 10485760
  133.8 0.7 copy.48
  134.5 0.6 copy.49
  135.1 0.6 copy.50
  135.8 0.6 copy.51
  136.4 0.6 copy.52
  137.0 0.8 copy.53
  137.8 0.8 copy.54
  138.6 0.5 copy.55
  139.1 0.5 copy.56
  139.6 0.5 copy.57
  140.2 0.5 copy.58
  140.7 0.5 copy.59
  141.2 0.5 copy.60
  (18 shorter events, 0.0 us)
Async XLA Ops:
  128.2 5.6 %copy-start.2 = (bf16[2,64,1024]{2,1,0:T(8,128)(2,1)S(1)}, bf16[2,64,1024]{2,1,0:T(8,128)(2,1)}, u32[]{:S(2)}) copy-start(bf16[2,64,1024]{2,1,0:T(8,128)(2,1)} %get-tuple-element.62) | copy-start | bytes 786436
  128.2 6.3 %copy-start.6 = (f32[128,128]{1,0:T(8,128)S(1)}, f32[128,128]{1,0:T(8,128)}, u32[]{:S(2)}) copy-start(f32[128,128]{1,0:T(8,128)} %get-tuple-element.63) | copy-start | bytes 196612
  128.2 7.0 %copy-start.5 = (f32[128,128]{1,0:T(8,128)S(1)}, f32[128,128]{1,0:T(8,128)}, u32[]{:S(2)}) copy-start(f32[128,128]{1,0:T(8,128)} %get-tuple-element.64) | copy-start | bytes 196612
  128.2 7.6 %copy-start.4 = (f32[128,128]{1,0:T(8,128)S(1)}, f32[128,128]{1,0:T(8,128)}, u32[]{:S(2)}) copy-start(f32[128,128]{1,0:T(8,128)} %get-tuple-element.65) | copy-start | bytes 196612
  128.2 8.2 %copy-start.3 = (f32[128,128]{1,0:T(8,128)S(1)}, f32[128,128]{1,0:T(8,128)}, u32[]{:S(2)}) copy-start(f32[128,128]{1,0:T(8,128)} %get-tuple-element.66) | copy-start | bytes 196612
  128.2 8.8 %copy-start.1 = (f32[128,1024]{1,0:T(8,128)S(1)}, f32[128,1024]{1,0:T(8,128)}, u32[]{:S(2)}) copy-start(f32[128,1024]{1,0:T(8,128)} %get-tuple-element.67) | copy-start | bytes 1572868
  128.2 9.6 %copy-start = (f32[1024,128]{1,0:T(8,128)S(1)}, f32[1024,128]{1,0:T(8,128)}, u32[]{:S(2)}) copy-start(f32[1024,128]{1,0:T(8,128)} %get-tuple-element.68) | copy-start | bytes 1572868
  128.2 10.4 %copy-start.12 = (f32[1,128]{1,0:T(1,128)S(1)}, f32[1,128]{1,0:T(1,128)}, u32[]{:S(2)}) copy-start(f32[1,128]{1,0:T(1,128)} %get-tuple-element.39) | copy-start | bytes 1540
  128.2 10.9 %copy-start.11 = (f32[1,128]{1,0:T(1,128)S(1)}, f32[1,128]{1,0:T(1,128)}, u32[]{:S(2)}) copy-start(f32[1,128]{1,0:T(1,128)} %get-tuple-element.40) | copy-start | bytes 1540
  128.2 11.4 %copy-start.10 = (f32[1,128]{1,0:T(1,128)S(1)}, f32[1,128]{1,0:T(1,128)}, u32[]{:S(2)}) copy-start(f32[1,128]{1,0:T(1,128)} %get-tuple-element.41) | copy-start | bytes 1540
  128.2 11.9 %copy-start.9 = (f32[1,128]{1,0:T(1,128)S(1)}, f32[1,128]{1,0:T(1,128)}, u32[]{:S(2)}) copy-start(f32[1,128]{1,0:T(1,128)} %get-tuple-element.42) | copy-start | bytes 1540
  128.2 12.4 %copy-start.8 = (f32[1,128]{1,0:T(1,128)S(1)}, f32[1,128]{1,0:T(1,128)}, u32[]{:S(2)}) copy-start(f32[1,128]{1,0:T(1,128)} %get-tuple-element.43) | copy-start | bytes 1540
  128.2 12.9 %copy-start.7 = (f32[1,128]{1,0:T(1,128)S(1)}, f32[1,128]{1,0:T(1,128)}, u32[]{:S(2)}) copy-start(f32[1,128]{1,0:T(1,128)} %get-tuple-element.44) | copy-start | bytes 1540

commit v2 on v1

--- a/solution.py
+++ b/solution.py
@@ -16,7 +16,7 @@
 NN = (((1,), (0,)), ((), ()))
 NT = (((1,), (1,)), ((), ()))
 TN = (((0,), (0,)), ((), ()))
-SEMS = 160
+SEMS = 112
 
 
 def dot(a, b, dims):
@@ -87,18 +87,10 @@
     lat_out,
     media_out,
     lgrad_out,
-    gq,
-    gk,
-    gv,
-    go,
+    gmat,
     gup,
     gdown,
-    vec0,
-    vec1,
-    vec2,
-    vec3,
-    vec4,
-    vec5,
+    vecs,
     send_sem,
     recv_sem,
     local_sem,
@@ -144,7 +136,8 @@
     midg,
     lowb,
     mgr,
-    kvg,
+    kg,
+    vg,
     qg,
     cgs,
     cgr,
@@ -159,6 +152,11 @@
     mgo,
     outl,
     outg,
+    wsc,
+    gupv,
+    gdnv,
+    gmv,
+    vsum,
     vgs,
     vgc,
     vgt,
@@ -187,7 +185,10 @@
     wire = Wire(send_sem, recv_sem)
 
     def w3b(ii, xx, cc):
-        return w3.at[xx, ii, :, at(cc * 384, 128 * 3)]
+        return w3.at[xx, ii // 2, ii % 2, :, :, at(cc * 128, 128)]
+
+    def w3col(xx, y_, cc):
+        return w3.at[xx, :, y_, :, :, at(cc * 128, 128)]
 
     local = []
 
@@ -197,9 +198,9 @@
         local.append(copy)
         return copy
 
-    bring(wk, w3.at[x, i, :, at(c * 384, 128)])
-    bring(wv, w3.at[x, i, :, at(c * 384 + 128, 128)])
-    bring(wq, w3.at[x, i, :, at(c * 384 + 256, 128)])
+    bring(wk, w3.at[x, z, yy, 0, :, at(c * 128, 128)])
+    bring(wv, w3.at[x, z, yy, 1, :, at(c * 128, 128)])
+    bring(wq, w3.at[x, z, yy, 2, :, at(c * 128, 128)])
     bring(wo, wob.at[j, :, at(i * 128, 128)])
     in_lat = bring(latents.at[c], lat)
     in_media = bring(media.at[c], xin)
@@ -216,92 +217,95 @@
     partners += [(peer(k), jx) for k in range(1, 4)]
     for dev in partners:
         pl.semaphore_signal(barrier, inc=1, device_id=dev, device_id_type=MESH)
-    pl.semaphore_wait(barrier, len(partners))
-
-    got_prm = [wire.send(prm_own, prm.at[i], (peer(k), j)) for k in range(1, 8)]
-    for copy in local[:4]:
-        copy.wait()
-
-    def wo_at(ii, jj):
-        return wob.at[jj, :, at(ii * 128, 128)]
-
-    def same(view, dev):
-        return wire.send(view, view, dev)
-
-    z3 = [same(w3b(i, x, c), (peer(2 * k), j)) for k in (1, 2, 3)]
-    y3 = [same(w3b(i, x, c), ypart)]
-    x3 = [same(w3b(i, x, c), xpart)]
-    zo = [same(wo_at(i, j), (peer(2 * k), j)) for k in (1, 2, 3)]
-    yo = [same(wo_at(i, j), ypart)]
-    xo = [same(wo_at(i, j), xpart)]
-
-    for copy in got_prm:
-        copy.wait_recv()
-    for ii in range(8):
-        vec[:, ii * 128 : (ii + 1) * 128] = prm[ii]
 
     in_lat.wait()
     lat32 = lat[...].astype(F32)
     lmean = jnp.mean(lat32, axis=-1, keepdims=True)
     lcen = lat32 - lmean
-    lrs = lax.rsqrt(jnp.mean(lcen * lcen, axis=-1, keepdims=True) + EPS)
-    kin[1280:1344, :] = (lcen * lrs * vec[2:3, :] + vec[3:4, :]).astype(BF16)
     mu[1280:1344, :] = lmean
-    rs[1280:1344, :] = lrs
+    rs[1280:1344, :] = lax.rsqrt(jnp.mean(lcen * lcen, axis=-1, keepdims=True) + EPS)
     in_media.wait()
+
+    def stat(t, carry):
+        rows = at(t * 64, 64)
+        v = xin[rows, :].astype(F32)
+        m = jnp.mean(v, axis=-1, keepdims=True)
+        cen = v - m
+        mu[rows, :] = m
+        rs[rows, :] = lax.rsqrt(jnp.mean(cen * cen, axis=-1, keepdims=True) + EPS)
+        return carry
+
+    lax.fori_loop(0, 20, stat, 0, unroll=4)
+    pl.semaphore_wait(barrier, len(partners))
+
+    got_prm = [wire.send(prm_own, prm.at[i], (peer(k), j)) for k in range(1, 8)]
+    for copy in local[:4]:
+        copy.wait()
+
+    def wo_at(ii, jj):
+        return wob.at[jj, :, at(ii * 128, 128)]
+
+    def same(view, dev):
+        return wire.send(view, view, dev)
+
+    z3 = [same(w3b(i, x, c), (peer(2 * k), j)) for k in (1, 2, 3)]
+    y3 = [same(w3b(i, x, c), ypart)]
+    zo = [same(wo_at(i, j), (peer(2 * k), j)) for k in (1, 2, 3)]
+    yo = [same(wo_at(i, j), ypart)]
+    for copy in got_prm:
+        copy.wait_recv()
+    for ii in range(8):
+        vec[:, ii * 128 : (ii + 1) * 128] = prm[ii]
 
     def media_norm(lo, hi):
         def strip(t, carry):
-            rows = at(t * 16, 16)
-            v = xin[rows, :].astype(F32)
-            m = jnp.mean(v, axis=-1, keepdims=True)
-            cen = v - m
-            rr = lax.rsqrt(jnp.mean(cen * cen, axis=-1, keepdims=True) + EPS)
-            kin[rows, :] = (cen * rr * vec[0:1, :] + vec[1:2, :]).astype(BF16)
-            mu[rows, :] = m
-            rs[rows, :] = rr
+            rows = at(t * 64, 64)
+            v = (xin[rows, :].astype(F32) - mu[rows, :]) * rs[rows, :]
+            kin[rows, :] = (v * vec[0:1, :] + vec[1:2, :]).astype(BF16)
             return carry
 
-        lax.fori_loop(lo, hi, strip, 0)
-
-    media_norm(0, 40)
+        lax.fori_loop(lo, hi, strip, 0, unroll=2)
+
+    kin[1280:1344, :] = (
+        (lat[...].astype(F32) - mu[1280:1344, :]) * rs[1280:1344, :] * vec[2:3, :] + vec[3:4, :]
+    ).astype(BF16)
+    media_norm(0, 10)
     for k in (1, 2, 3):
         z3[k - 1].wait_recv()
         y3.append(same(w3b(peer(2 * k), x, c), ypart))
-        x3.append(same(w3b(peer(2 * k), x, c), xpart))
+    c3 = [same(w3col(x, yy, c), cpart)]
+    x3 = [same(w3col(x, yy, c), xpart)]
+    for k in (1, 2, 3):
+        zo[k - 1].wait_recv()
+        yo.append(same(wo_at(peer(2 * k), j), ypart))
     in_cot.wait()
     cots = [wire.send(cota.at[r], cota.at[r], (peer(k), j)) for k in (1, 2, 3)]
     ups, dns = [], []
-    for k in range(1, 8):
+    for k in (4, 5, 6, 7, 2, 3, 1):
         rk = peer(k) % 4
         ups.append(
             wire.send(
                 up.at[:, at(rk * 256, 256)], upb.at[i, :, at(c * 256, 256)], (peer(k), j)
             )
         )
-    for k in range(1, 8):
+    for k in (4, 5, 6, 7, 2, 3, 1):
         rk = peer(k) % 4
         dns.append(
             wire.send(
                 down.at[at(rk * 256, 256), :], dnb.at[c, :, at(i * 128, 128)], (peer(k), j)
             )
         )
-    media_norm(40, 60)
-    for k in (0, 1, 2, 3):
-        y3[k].wait_recv()
-        x3.append(same(w3b(peer(2 * k + 1), x, c), xpart))
-    own3 = w3.at[x, :, :, at(c * 384, 128 * 3)]
-    c3 = same(own3, cpart)
-    for k in (1, 2, 3):
-        zo[k - 1].wait_recv()
-        yo.append(same(wo_at(peer(2 * k), j), ypart))
-        xo.append(same(wo_at(peer(2 * k), j), xpart))
-    media_norm(60, 80)
-    for k in (0, 1, 2, 3):
-        yo[k].wait_recv()
-        xo.append(same(wo_at(peer(2 * k + 1), j), xpart))
+    media_norm(10, 20)
+    for copy in y3:
+        copy.wait_recv()
+    c3.append(same(w3col(x, 1 - yy, c), cpart))
+    for copy in yo:
+        copy.wait_recv()
+    xo = same(wob.at[j], xpart)
     co = same(wob.at[j], cpart)
-    c3.wait_recv()
+    x3.append(same(w3col(x, 1 - yy, c), xpart))
+    for copy in c3:
+        copy.wait_recv()
 
     count = counts[c]
     head_of_lane = lax.broadcasted_iota(jnp.int32, (256, 256), 1) // HEAD
@@ -319,81 +323,53 @@
             out = jnp.where(lane64 == h, v[h * 64 : (h + 1) * 64, :], out)
         return out
 
-    def w_kv(g, cc):
-        return w3[g, :, :, cc * 384 : cc * 384 + 256].reshape(1024, 256)
-
-    def w_q(g, cc):
-        return w3[g, :, :, cc * 384 + 256 : cc * 384 + 384].reshape(1024, 128)
-
-    def attention(g):
-        def project(t, carry):
-            rows = at(t * 448, 448)
-            a = kin[rows, :]
-            for cc in (0, 1):
-                o = dot(a, w_kv(g, cc), NN)
-                kb[g, rows, cc * 128 : (cc + 1) * 128] = o[:, :128].astype(BF16)
-                vb[g, rows, cc * 128 : (cc + 1) * 128] = o[:, 128:].astype(BF16)
-            return carry
-
-        lax.fori_loop(0, 3, project, 0)
-        for cc in (0, 1):
-            qb[g, :, cc * 128 : (cc + 1) * 128] = dot(
-                kin[1280:1344, :], w_q(g, cc), NN
-            ).astype(BF16)
-        q4 = spread(qb[g])
-
-        def score(t, top):
-            rows = at(t * 192, 192)
-            s = dot(kb[g, rows, :], q4, NT) * 0.125
-            key = lax.broadcasted_iota(jnp.int32, (192, 256), 0) + t * 192
-            ok = jnp.logical_or(key < count * PATCH, key >= 1280)
-            s = jnp.where(ok, s, -1e30)
-            att[g, rows, :] = s
-            return jnp.maximum(top, jnp.max(s, axis=0, keepdims=True))
-
-        top = lax.fori_loop(0, 7, score, jnp.full((1, 256), -1e30, F32))
-
-        def raise_(t, total):
-            rows = at(t * 64, 64)
-            e = jnp.exp(att[g, rows, :] - top)
-            att[g, rows, :] = e
-            return total + jnp.sum(e, axis=0, keepdims=True)
-
-        total = lax.fori_loop(0, 21, raise_, jnp.zeros((1, 256), F32))
-        scale = 1.0 / total
-
-        def level(t, carry):
-            rows = at(t * 64, 64)
-            p = att[g, rows, :] * scale
-            att[g, rows, :] = p
-            attl[g, rows, :] = p.astype(BF16)
-            return carry
-
-        lax.fori_loop(0, 21, level, 0)
-        mixed = dot(attl[g], vb[g], TN)
-        mix[:, at(g * 256, 256)] = gather_heads(mixed).astype(BF16)
+    def weight(g, m):
+        return w3[g, :, :, m].reshape(1024, 256)
+
+    def attention(g, mixing=True):
+        a = kin[...]
+        kb[g] = dot(a, weight(g, 0), NN).astype(BF16)
+        vb[g] = dot(a, weight(g, 1), NN).astype(BF16)
+        qb[g] = dot(kin[1280:1344, :], weight(g, 2), NN).astype(BF16)
+        s = dot(kb[g], spread(qb[g]), NT) * 0.125
+        key = lax.broadcasted_iota(jnp.int32, (1344, 256), 0)
+        s = jnp.where(jnp.logical_or(key < count * PATCH, key >= 1280), s, -1e30)
+        att[g] = s
+        top = jnp.max(s, axis=0, keepdims=True)
+        e = jnp.exp(att[g] - top)
+        att[g] = e
+        scale = 1.0 / jnp.sum(e, axis=0, keepdims=True)
+        p = att[g] * scale
+        att[g] = p
+        attl[g] = p.astype(BF16)
+        if mixing:
+            mixed = dot(attl[g], vb[g], TN)
+            mix[g] = gather_heads(mixed).astype(BF16)
 
     attention(x)
-    for copy in x3:
-        copy.wait_recv()
-    oth3 = w3.at[ox, :, :, at(c * 384, 128 * 3)]
-    c3b = same(oth3, cpart)
-    for copy in xo:
-        copy.wait_recv()
+    mx = same(mix.at[x], xpart)
+    xo.wait_recv()
     cob = same(wob.at[jx], cpart)
-    c3b.wait_recv()
-    attention(ox)
+    mx.wait_recv()
     co.wait_recv()
     cob.wait_recv()
 
     wo_all = wob[...].reshape(512, 1024)
-    middle = lat[...].astype(F32) + dot(mix[...], wo_all, NN)
+    middle = lat[...].astype(F32) + dot(jnp.concatenate([mix[0], mix[1]], axis=1), wo_all, NN)
     mid[...] = middle
     fmean = jnp.mean(middle, axis=-1, keepdims=True)
     fcen = middle - fmean
     frs = lax.rsqrt(jnp.mean(fcen * fcen, axis=-1, keepdims=True) + EPS)
     hid[r] = (fcen * frs * vec[4:5, :] + vec[5:6, :]).astype(BF16)
     hids = [wire.send(hid.at[r], hid.at[r], (peer(k), j)) for k in (3, 2, 1)]
+
+    c3b = []
+    for copy, y_ in zip(x3, (yy, 1 - yy)):
+        copy.wait_recv()
+        c3b.append(same(w3col(ox, y_, c), cpart))
+    for copy in c3b:
+        copy.wait_recv()
+    attention(ox, False)
 
     in_up.wait()
     in_dn.wait()
@@ -497,68 +473,59 @@
         mgr[g] = mgr_all[:, g * 256 : (g + 1) * 256]
     lowb[...] = low
 
-    def back(g):
+    def back_values(g):
         m4 = spread(mgr[g])
+
+        vg[g] = dot(attl[g], m4, NN).astype(BF16)
+        pa = att[g] * dot(vb[g], m4, NT)
+        dxs[:, 0:256] = pa
+        return jnp.sum(pa, axis=0, keepdims=True)
+
+    def back_keys(g, delta):
         q4 = spread(qb[g])
 
-        def first(t, delta):
-            rows = at(t * 192, 192)
-            vg = dot(attl[g, rows, :], m4, NN).astype(BF16)
-            kvg[rows, at(g * 512 + 128, 128)] = vg[:, :128]
-            kvg[rows, at(g * 512 + 384, 128)] = vg[:, 128:]
-            ag = dot(vb[g, rows, :], m4, NT)
-            pa = att[g, rows, :] * ag
-            dxs[rows, 0:256] = pa
-            return delta + jnp.sum(pa, axis=0, keepdims=True)
-
-        delta = lax.fori_loop(0, 7, first, jnp.zeros((1, 256), F32))
-
-        def second(t, total):
-            rows = at(t * 192, 192)
-            sg = (dxs[rows, 0:256] - att[g, rows, :] * delta).astype(BF16)
-            kg = (dot(sg, q4, NN) * 0.125).astype(BF16)
-            kvg[rows, at(g * 512, 128)] = kg[:, :128]
-            kvg[rows, at(g * 512 + 256, 128)] = kg[:, 128:]
-            return total + dot(sg, kb[g, rows, :], TN)
-
-        total = lax.fori_loop(0, 7, second, jnp.zeros((256, 256), F32))
+        sg = (dxs[:, 0:256] - att[g] * delta).astype(BF16)
+        attl[g] = sg
+        kg[g] = (dot(sg, q4, NN) * 0.125).astype(BF16)
+        total = dot(attl[g], kb[g], TN)
         qg[g] = (gather_heads(total) * 0.125).astype(BF16)
 
-    back(x)
-    def weight_tile(t, carry):
-        cols = at(t * 256, 256)
-        two = pl.ds(t * 2, 2)
-        o = dot(kin[:, cols], kvg[:, at(x * 512 + oc * 256, 256)], TN)
-        cgs[two, :, 0:256] = o.astype(BF16).reshape(2, 128, 256)
-        gown[cols, 0:256] = dot(kin[:, cols], kvg[:, at(x * 512 + c * 256, 256)], TN)
-        return carry
-
-    lax.fori_loop(0, 4, weight_tile, 0)
-
-    def small_tile(t, carry):
-        cols = at(t * 256, 256)
-        dxs[cols, 0:256] = dot(kin[1280:1344, cols], qg[x], TN)
-        dxs[cols, 256:512] = dot(lowb[:, cols], mix[:, at(x * 256, 256)], TN)
-        return carry
-
-    lax.fori_loop(0, 4, small_tile, 0)
-    gown[:, 256:384] = dxs[0:1024, at(c * 128, 128)]
-    gown[:, 384:512] = dxs[0:1024, at(256 + c * 128, 128)]
-    cgs[:, :, 256:384] = dxs[0:1024, at(oc * 128, 128)].astype(BF16).reshape(8, 128, 128)
-    cgs[:, :, 384:512] = dxs[0:1024, at(256 + oc * 128, 128)].astype(BF16).reshape(8, 128, 128)
-    cg_in = wire.send(cgs, cgr, cpart)
-
-    back(ox)
-
-    cg_in.wait_recv()
-    g1[...] = (
-        (gown[...].reshape(8, 128, 512) + cgr[...].astype(F32)).astype(BF16).reshape(4, 2, 128, 512)
-    )
-    y_in = wire.send(g1.at[:, 1 - yy], yr, ypart)
+    def split(m, wide):
+        wsc[...] = wide
+        mine, other = wsc[at(c * 128, 128), :], wsc[at(oc * 128, 128), :]
+        for ii in range(8):
+            cols = slice(ii * 128, (ii + 1) * 128)
+            gown[ii // 2, ii % 2, m] = mine[:, cols]
+            cgs[ii // 2, ii % 2, m] = other[:, cols].astype(BF16)
+
+    def two(ref, p):
+        return ref.at[:, :, 2 * p : 2 * p + 2]
+
+    def chip_sum(p):
+        two(g1, p)[...] = (two(gown, p)[...] + two(cgr, p)[...].astype(F32)).astype(BF16)
+        return wire.send(g1.at[:, 1 - yy, 2 * p : 2 * p + 2], yr.at[:, 2 * p : 2 * p + 2], ypart)
+
+    delta = back_values(x)
+    split(0, dot(vg[x], kin[...], TN))
+    split(1, dot(mix[x], lowb[...], TN))
+    cg_in = [wire.send(two(cgs, 0), two(cgr, 0), cpart)]
+    back_keys(x, delta)
+    split(2, dot(kg[x], kin[...], TN))
+    split(3, dot(qg[x], kin[1280:1344, :], TN))
+    cg_in.append(wire.send(two(cgs, 1), two(cgr, 1), cpart))
+    y_in = []
+    for p in (0, 1):
+        cg_in[p].wait_recv()
+        y_in.append(chip_sum(p))
+    back_keys(ox, back_values(ox))
 
     def dx_tile(rows):
-        w_all = jnp.concatenate([w_kv(0, 0), w_kv(0, 1), w_kv(1, 0), w_kv(1, 1)], axis=1)
-        return dot(kvg[rows, :], w_all, NT)
+        return (
+            dot(kg[0, rows, :], weight(0, 0), NT)
+            + dot(kg[1, rows, :], weight(1, 0), NT)
+            + dot(vg[0, rows, :], weight(0, 1), NT)
+            + dot(vg[1, rows, :], weight(1, 1), NT)
+        )
 
     accg[...] = jnp.zeros((8, 1024), F32)
     accb[...] = jnp.zeros((8, 1024), F32)
@@ -577,30 +544,36 @@
     def media_back(t, carry):
         dxs[0:256, :] = dx_tile(at(t * 256, 256))
 
-        def strip(u, carry):
-            here = at(u * 16, 16)
-            rows = at(t * 256 + u * 16, 16)
-            v = xin[rows, :].astype(F32)
-            dy = dxs[here, :]
-            dz, zhat = norm_back(v, mu[rows, :], rs[rows, :], vec[0:1, :], dy)
-            mgo[rows, :] = dz.astype(BF16)
-            pz = dy * zhat
-            accg[...] += pz[0:8, :] + pz[8:16, :]
-            accb[...] += dy[0:8, :] + dy[8:16, :]
-            return carry
-
-        lax.fori_loop(0, 16, strip, 0)
+        rows = at(t * 256, 256)
+        v = xin[rows, :].astype(F32)
+        dy = dxs[0:256, :]
+        dz, zhat = norm_back(v, mu[rows, :], rs[rows, :], vec[0:1, :], dy)
+        mgo[rows, :] = dz.astype(BF16)
+        accg[...] += (dy * zhat).reshape(32, 8, 1024).sum(0)
+        accb[...] += dy.reshape(32, 8, 1024).sum(0)
         out_copy(t, out_base + t).start()
         keep_copy(t).start()
         return carry
 
-    lax.fori_loop(0, 5, media_back, 0)
+    def pass_on(p):
+        y_in[p].wait_recv()
+        here = slice(2 * p, 2 * p + 2)
+        g2[:, here] = (g1[:, yy, here].astype(F32) + yr[:, here].astype(F32)).astype(BF16)
+        zr[z, here] = g2[z, here]
+        return [
+            wire.send(g2.at[peer(2 * k) // 2, here], zr.at[z, here], (peer(2 * k), j))
+            for k in (2, 3, 1)
+        ]
+
+    lax.fori_loop(0, 1, media_back, 0)
+    z_in = pass_on(0)
+    lax.fori_loop(1, 3, media_back, 0)
+    z_in += pass_on(1)
+    lax.fori_loop(3, 5, media_back, 0)
     put_vec(0, jnp.sum(accg[...], axis=0, keepdims=True))
     put_vec(1, jnp.sum(accb[...], axis=0, keepdims=True))
     dxs[0:64, :] = dx_tile(pl.ds(1280, 64))
-    q_all = jnp.concatenate([qg[0], qg[1]], axis=1)
-    wq_all = jnp.concatenate([w_q(0, 0), w_q(0, 1), w_q(1, 0), w_q(1, 1)], axis=1)
-    lsum = dxs[0:64, :] + dot(q_all, wq_all, NT)
+    lsum = dxs[0:64, :] + dot(qg[0], weight(0, 2), NT) + dot(qg[1], weight(1, 2), NT)
     lat32 = lat[...].astype(F32)
     dz, zhat = norm_back(lat32, mu[1280:1344, :], rs[1280:1344, :], vec[2:3, :], lsum)
     outg[...] = (midg[...] + dz).astype(BF16)
@@ -613,12 +586,6 @@
         vgs[ii, 6:8, :] = jnp.zeros((2, 128), F32)
     vg_in = wire.send(vgs, vgc, cpart)
 
-    y_in.wait_recv()
-    total = g1[:, yy].astype(F32) + yr[...].astype(F32)
-    g2[...] = total.astype(BF16)
-    z_in = [wire.send(g2.at[peer(2 * k) // 2], zr.at[z], (peer(2 * k), j)) for k in (1, 2, 3)]
-    zr[z] = g2[z]
-
     vg_in.wait_recv()
     vgt[...] = vgs[...] + vgc[...]
     vga[i] = vgt[i]
@@ -633,11 +600,15 @@
     for copy in gu_out:
         copy.wait_recv()
     for q in range(4):
-        gup[:, q * 256 : (q + 1) * 256] = gua[q].astype(F32) + gua[4 + q].astype(F32)
+        gupv[:, q * 256 : (q + 1) * 256] = gua[q].astype(F32) + gua[4 + q].astype(F32)
+    gup_keep = pltpu.make_async_copy(gupv, gup, local_sem.at[27])
+    gup_keep.start()
     for copy in gd_out:
         copy.wait_recv()
     for q in range(4):
-        gdown[q * 256 : (q + 1) * 256, :] = gda[q].astype(F32) + gda[4 + q].astype(F32)
+        gdnv[q * 256 : (q + 1) * 256, :] = gda[q].astype(F32) + gda[4 + q].astype(F32)
+    gdn_keep = pltpu.make_async_copy(gdnv, gdown, local_sem.at[28])
+    gdn_keep.start()
 
     fox_in.wait_recv()
     outl[...] = (mid[...] + fox[...].reshape(64, 1024).astype(F32)).astype(BF16)
@@ -648,15 +619,17 @@
     for copy in z_in:
         copy.wait_recv()
     last = sum_of(zr, 4)
-    gk[...] = last[:, 0:128]
-    gv[...] = last[:, 128:256]
-    gq[...] = last[:, 256:384]
-    go[...] = last[:, 384:512].T
+    gmv[0] = last[3].T
+    gmv[1] = last[2].T
+    gmv[2] = last[0].T
+    gmv[3] = last[1]
+    gm_keep = pltpu.make_async_copy(gmv, gmat, local_sem.at[29])
+    gm_keep.start()
     for copy in v_in:
         copy.wait_recv()
-    sums = sum_of(vga, 8)
-    for k, ref in enumerate((vec0, vec1, vec2, vec3, vec4, vec5)):
-        ref[...] = sums[k : k + 1, :]
+    vsum[...] = sum_of(vga, 8)
+    v_keep = pltpu.make_async_copy(vsum, vecs, local_sem.at[30])
+    v_keep.start()
 
     for t in range(5):
         keep_copy(t).wait()
@@ -665,6 +638,10 @@
         out.wait_recv()
     lg_keep.wait()
     lo_keep.wait()
+    gup_keep.wait()
+    gdn_keep.wait()
+    gm_keep.wait()
+    v_keep.wait()
     lg_in.wait_recv()
     lo_in.wait_recv()
     wire.drain()
@@ -679,7 +656,7 @@
     ("kin", (1344, 1024), BF16),
     ("mu", (1344, 1), F32),
     ("rs", (1344, 1), F32),
-    ("w3", (2, 8, 128, 768), BF16),
+    ("w3", (2, 4, 2, 3, 128, 256), BF16),
     ("wob", (4, 128, 1024), BF16),
     ("upb", (8, 128, 512), BF16),
     ("dnb", (2, 256, 1024), BF16),
@@ -688,7 +665,7 @@
     ("qb", (2, 64, 256), BF16),
     ("att", (2, 1344, 256), F32),
     ("attl", (2, 1344, 256), BF16),
-    ("mix", (64, 512), BF16),
+    ("mix", (2, 64, 256), BF16),
     ("mid", (64, 1024), F32),
     ("hid", (4, 64, 1024), BF16),
     ("cota", (4, 64, 1024), BF16),
@@ -713,26 +690,62 @@
     ("midg", (64, 1024), F32),
     ("lowb", (64, 1024), BF16),
     ("mgr", (2, 64, 256), BF16),
-    ("kvg", (1344, 1024), BF16),
+    ("kg", (2, 1344, 256), BF16),
+    ("vg", (2, 1344, 256), BF16),
     ("qg", (2, 64, 256), BF16),
-    ("cgs", (8, 128, 512), BF16),
-    ("cgr", (8, 128, 512), BF16),
-    ("gown", (1024, 512), F32),
-    ("g1", (4, 2, 128, 512), BF16),
-    ("yr", (4, 128, 512), BF16),
-    ("g2", (4, 128, 512), BF16),
-    ("zr", (4, 128, 512), BF16),
+    ("cgs", (4, 2, 4, 128, 128), BF16),
+    ("cgr", (4, 2, 4, 128, 128), BF16),
+    ("gown", (4, 2, 4, 128, 128), F32),
+    ("g1", (4, 2, 4, 128, 128), BF16),
+    ("yr", (4, 4, 128, 128), BF16),
+    ("g2", (4, 4, 128, 128), BF16),
+    ("zr", (4, 4, 128, 128), BF16),
     ("dxs", (1344, 1024), F32),
     ("accg", (8, 1024), F32),
     ("accb", (8, 1024), F32),
     ("mgo", (1280, 1024), BF16),
     ("outl", (64, 1024), BF16),
     ("outg", (64, 1024), BF16),
+    ("wsc", (256, 1024), F32),
+    ("gupv", (128, 1024), F32),
+    ("gdnv", (1024, 128), F32),
+    ("gmv", (4, 128, 128), F32),
+    ("vsum", (8, 128), F32),
     ("vgs", (8, 8, 128), F32),
     ("vgc", (8, 8, 128), F32),
     ("vgt", (8, 8, 128), F32),
     ("vga", (8, 8, 128), F32),
 )
+
+
+CHUNKS = 10
+
+
+def hand_out(lat, med, lgr, gmat, gup, gdown, vecs, *rest):
+    outs, (v_lat, v_med, v_lgr, v_gmat, v_gup, v_gdown, v_vecs, sem_in, sem_out) = rest[:15], rest[15:]
+    rows = med.shape[0] * med.shape[1] // CHUNKS
+    per = med.shape[1] // rows
+    moves = []
+    for k in range(CHUNKS):
+        part = (k // per, pl.ds((k % per) * rows, rows))
+        moves.append((med.at[part], v_med.at[part], [(v_med.at[part], outs[1].at[part])]))
+    moves.append((gup, v_gup, [(v_gup, outs[7])]))
+    moves.append((gdown, v_gdown, [(v_gdown, outs[8])]))
+    moves.append((lat, v_lat, [(v_lat, outs[0])]))
+    moves.append((lgr, v_lgr, [(v_lgr, outs[2])]))
+    moves.append((gmat, v_gmat, [(v_gmat.at[k], outs[3 + k]) for k in range(4)]))
+    moves.append((vecs, v_vecs, [(v_vecs.at[k : k + 1], outs[9 + k]) for k in range(6)]))
+    first = [pltpu.make_async_copy(a, b, sem_in.at[k]) for k, (a, b, _) in enumerate(moves)]
+    for copy in first:
+        copy.start()
+    second = []
+    for copy, (_, _, then) in zip(first, moves):
+        copy.wait()
+        for a, b in then:
+            second.append(pltpu.make_async_copy(a, b, sem_out.at[len(second)]))
+            second[-1].start()
+    for copy in second:
+        copy.wait()
 
 
 def fused(media, latents, cotangent, image_counts, wq, wk, wv, wo, up, down, *gains):
@@ -746,16 +759,13 @@
             shape(latents.shape, BF16),
             shape(media.shape, BF16),
             shape(latents.shape, BF16),
-            shape(wq.shape, F32),
-            shape(wk.shape, F32),
-            shape(wv.shape, F32),
-            shape(wo.shape, F32),
+            shape((4, 128, 128), F32),
             shape(up.shape, F32),
             shape(down.shape, F32),
-        ]
-        + [shape((1, 128), F32)] * 6,
+            shape((8, 128), F32),
+        ],
         in_specs=[smem] + [anyspace] * 9 + [vmem] * 6,
-        out_specs=[anyspace] * 3 + [vmem] * 12,
+        out_specs=[anyspace] * 7,
         scratch_shapes=[
             pltpu.SemaphoreType.DMA((SEMS,)),
             pltpu.SemaphoreType.DMA((SEMS,)),
@@ -781,6 +791,17 @@
         down,
         *[v.reshape(1, 128) for v in gains],
     )
+    outs = pl.pallas_call(
+        hand_out,
+        out_shape=[shape(v.shape, v.dtype) for v in outs[:3]]
+        + [shape(v.shape, F32) for v in (wq, wk, wv, wo, up, down)]
+        + [shape((1, 128), F32)] * 6,
+        in_specs=[anyspace] * 7,
+        out_specs=[anyspace] * 15,
+        scratch_shapes=[pltpu.VMEM(v.shape, v.dtype) for v in outs]
+        + [pltpu.SemaphoreType.DMA((CHUNKS + 6,)), pltpu.SemaphoreType.DMA((CHUNKS + 14,))],
+        compiler_params=pltpu.CompilerParams(vmem_limit_bytes=60 * 2**20),
+    )(*outs)
     return tuple(outs[:9]) + tuple(v.reshape(128) for v in outs[9:])
 
 

time: 142 us -> 107 us (0.75)
  Pallas kernels: 126 us -> 106 us
  local copies, waits for them, and re-layouts: 15.1 us -> 0 us
    pallas_call x1, Pallas kernels: 126 us -> 100 us  [fused(): pl.pallas_call(layer_kernel, out_shape=[shape(latents.shape, BF16), shape...]
    unnamed x41 -> x0, local copies, waits for them, and re-layouts: 15.1 us -> none
    pallas_call x0 -> x1, Pallas kernels: none -> 5.84 us  [fused(): pl.pallas_call(hand_out, out_shape=[shape(v.shape, v.dtype) for v in outs...]
where the time goes in v2:
time: 107 us
  Pallas kernels  106 us (99%)
    pallas_call x1, Pallas kernels, fused(): pl.pallas_call(layer_kernel, out_shape=[shape(latents.shape, BF16), shape...  100 us
    pallas_call x1, Pallas kernels, fused(): pl.pallas_call(hand_out, out_shape=[shape(v.shape, v.dtype) for v in outs...  5.84 us

profile of v2, /device:TPU:0, one launch (start us, length us, event | category | flops | bytes accessed | tf_op | source)
XLA Modules:
  0.0 106.7 jit_solution(2402582862726139476)
XLA Ops:
  0.7 100.1 %shard_map.271 = (bf16[2,64,1024]{2,1,0:T(8,128)(2,1)}, bf16[2,1280,1024]{2,1,0:T(8,128)(2,1)}, bf16[2,64,1024]{2,1,0:T(8,128)(2,1)}, f32[4,128,128]{2,1,0:T(8,1...) custom-call(s32[2]{0:T(128)} %counts.1, bf16[2,1280,1024]{2,1,0:T(8,128)(2,1)} %media.1, ...), custom_call_target="tpu_custom_call" | custom-call | flops 14000000000 | bytes 20000000 | tf_op jit(solution)/shard_map/pallas_call | solution.py:756
  100.7 5.8 %shard_map.272 = (bf16[2,64,1024]{2,1,0:T(8,128)(2,1)}, bf16[2,1280,1024]{2,1,0:T(8,128)(2,1)}, bf16[2,64,1024]{2,1,0:T(8,128)(2,1)}, f32[128,128]{1,0:T(8,128)}...) custom-call(bf16[2,64,1024]{2,1,0:T(8,128)(2,1)} %get-tuple-element., ...), custom_call_target="tpu_custom_call" | custom-call | tf_op jit(solution)/shard_map/pallas_call | solution.py:794

commit v3 on v2

--- a/solution.py
+++ b/solution.py
@@ -16,7 +16,8 @@
 NN = (((1,), (0,)), ((), ()))
 NT = (((1,), (1,)), ((), ()))
 TN = (((0,), (0,)), ((), ()))
-SEMS = 112
+LIMIT = 54
+SEMS = 68
 
 
 def dot(a, b, dims):
@@ -51,6 +52,14 @@
     def send(self, src, dst, dev):
         copy = self.make(self.take(), src, dst, dev)
         copy.start()
+        self.sent.append(copy)
+        return copy
+
+    def send_all(self, parts, whole):
+        slot = self.take()
+        for src, dst, dev in parts:
+            self.make(slot, src, dst, dev).start()
+        copy = self.make(slot, whole, whole, parts[0][2])
         self.sent.append(copy)
         return copy
 
@@ -102,8 +111,8 @@
     kin,
     mu,
     rs,
-    w3,
-    wob,
+    w4,
+    wo_own,
     upb,
     dnb,
     kb,
@@ -121,6 +130,8 @@
     hgr,
     hgx,
     fos,
+    fxr,
+    fos2,
     fors,
     fox,
     gus,
@@ -146,17 +157,11 @@
     yr,
     g2,
     zr,
+    zs,
     dxs,
     accg,
     accb,
-    mgo,
-    outl,
-    outg,
     wsc,
-    gupv,
-    gdnv,
-    gmv,
-    vsum,
     vgs,
     vgc,
     vgt,
@@ -185,10 +190,12 @@
     wire = Wire(send_sem, recv_sem)
 
     def w3b(ii, xx, cc):
-        return w3.at[xx, ii // 2, ii % 2, :, :, at(cc * 128, 128)]
-
-    def w3col(xx, y_, cc):
-        return w3.at[xx, :, y_, :, :, at(cc * 128, 128)]
+        return w4.at[xx, ii // 2, ii % 2, :, :, at(cc * 128, 128)]
+
+    out_w, kqv = slice(3, 4), slice(0, 3)
+
+    def w3col(xx, y_, cc, mats=kqv):
+        return w4.at[xx, :, y_, mats, :, at(cc * 128, 128)]
 
     local = []
 
@@ -198,10 +205,10 @@
         local.append(copy)
         return copy
 
-    bring(wk, w3.at[x, z, yy, 0, :, at(c * 128, 128)])
-    bring(wv, w3.at[x, z, yy, 1, :, at(c * 128, 128)])
-    bring(wq, w3.at[x, z, yy, 2, :, at(c * 128, 128)])
-    bring(wo, wob.at[j, :, at(i * 128, 128)])
+    bring(wk, w4.at[x, z, yy, 0, :, at(c * 128, 128)])
+    bring(wv, w4.at[x, z, yy, 1, :, at(c * 128, 128)])
+    bring(wq, w4.at[x, z, yy, 2, :, at(c * 128, 128)])
+    bring(wo, wo_own)
     in_lat = bring(latents.at[c], lat)
     in_media = bring(media.at[c], xin)
     in_cot = bring(cot.at[c], cota.at[r])
@@ -238,22 +245,19 @@
     lax.fori_loop(0, 20, stat, 0, unroll=4)
     pl.semaphore_wait(barrier, len(partners))
 
-    got_prm = [wire.send(prm_own, prm.at[i], (peer(k), j)) for k in range(1, 8)]
     for copy in local[:4]:
         copy.wait()
-
-    def wo_at(ii, jj):
-        return wob.at[jj, :, at(ii * 128, 128)]
+    w4[x, z, yy, 3, :, at(c * 128, 128)] = wo_own[...].astype(F32).T.astype(BF16)
+    others = range(1, 8)
+    got_prm = wire.send_all([(prm_own, prm.at[i], (peer(k), j)) for k in others], prm.at[0:7])
 
     def same(view, dev):
         return wire.send(view, view, dev)
 
-    z3 = [same(w3b(i, x, c), (peer(2 * k), j)) for k in (1, 2, 3)]
+    z_near = same(w3b(i, x, c), (peer(2), j))
+    z_far = same(w3b(i, x, c), (peer(4), j))
     y3 = [same(w3b(i, x, c), ypart)]
-    zo = [same(wo_at(i, j), (peer(2 * k), j)) for k in (1, 2, 3)]
-    yo = [same(wo_at(i, j), ypart)]
-    for copy in got_prm:
-        copy.wait_recv()
+    got_prm.wait_recv()
     for ii in range(8):
         vec[:, ii * 128 : (ii + 1) * 128] = prm[ii]
 
@@ -270,40 +274,38 @@
         (lat[...].astype(F32) - mu[1280:1344, :]) * rs[1280:1344, :] * vec[2:3, :] + vec[3:4, :]
     ).astype(BF16)
     media_norm(0, 10)
-    for k in (1, 2, 3):
-        z3[k - 1].wait_recv()
-        y3.append(same(w3b(peer(2 * k), x, c), ypart))
-    c3 = [same(w3col(x, yy, c), cpart)]
+    z_far.wait_recv()
+    z_relay = same(w3b(peer(4), x, c), (peer(2), j))
+    y3.append(same(w3b(peer(4), x, c), ypart))
+    z_near.wait_recv()
+    y3.append(same(w3b(peer(2), x, c), ypart))
+    z_relay.wait_recv()
+    y3.append(same(w3b(peer(6), x, c), ypart))
+    everything = slice(0, 4)
+    c3 = [same(w3col(x, yy, c, everything), cpart)]
+    xo = [same(w3col(x, yy, c, out_w), xpart)]
     x3 = [same(w3col(x, yy, c), xpart)]
-    for k in (1, 2, 3):
-        zo[k - 1].wait_recv()
-        yo.append(same(wo_at(peer(2 * k), j), ypart))
+    def up_part(k):
+        return up.at[:, at(peer(k) % 4 * 256, 256)], upb.at[i, :, at(c * 256, 256)], (peer(k), j)
+
+    def down_part(k):
+        return down.at[at(peer(k) % 4 * 256, 256), :], dnb.at[c, :, at(i * 128, 128)], (peer(k), j)
+
+    near, crossing = (4, 6, 2), (5, 7, 3, 1)
+    ups = [wire.send_all([up_part(k) for k in near], upb.at[0:3, :, 0:256])]
+    dns = [wire.send_all([down_part(k) for k in near], dnb.at[0, :, 0:384])]
+    ups.append(wire.send_all([up_part(k) for k in crossing], upb.at[0:4, :, 0:256]))
+    dns.append(wire.send_all([down_part(k) for k in crossing], dnb.at[0, :, 0:512]))
     in_cot.wait()
-    cots = [wire.send(cota.at[r], cota.at[r], (peer(k), j)) for k in (1, 2, 3)]
-    ups, dns = [], []
-    for k in (4, 5, 6, 7, 2, 3, 1):
-        rk = peer(k) % 4
-        ups.append(
-            wire.send(
-                up.at[:, at(rk * 256, 256)], upb.at[i, :, at(c * 256, 256)], (peer(k), j)
-            )
-        )
-    for k in (4, 5, 6, 7, 2, 3, 1):
-        rk = peer(k) % 4
-        dns.append(
-            wire.send(
-                down.at[at(rk * 256, 256), :], dnb.at[c, :, at(i * 128, 128)], (peer(k), j)
-            )
-        )
+    cots = wire.send_all(
+        [(cota.at[r], cota.at[r], (peer(k), j)) for k in (1, 2, 3)], cota.at[0:3]
+    )
+
     media_norm(10, 20)
     for copy in y3:
         copy.wait_recv()
-    c3.append(same(w3col(x, 1 - yy, c), cpart))
-    for copy in yo:
-        copy.wait_recv()
-    xo = same(wob.at[j], xpart)
-    co = same(wob.at[j], cpart)
-    x3.append(same(w3col(x, 1 - yy, c), xpart))
+    c3.append(same(w3col(x, 1 - yy, c, everything), cpart))
+    xo.append(same(w3col(x, 1 - yy, c, out_w), xpart))
     for copy in c3:
         copy.wait_recv()
 
@@ -324,7 +326,7 @@
         return out
 
     def weight(g, m):
-        return w3[g, :, :, m].reshape(1024, 256)
+        return w4[g, :, :, m].reshape(1024, 256)
 
     def attention(g, mixing=True):
         a = kin[...]
@@ -348,28 +350,22 @@
 
     attention(x)
     mx = same(mix.at[x], xpart)
-    xo.wait_recv()
-    cob = same(wob.at[jx], cpart)
+    x3.append(same(w3col(x, 1 - yy, c), xpart))
+    cob = []
+    for copy, y_ in zip(xo, (yy, 1 - yy)):
+        copy.wait_recv()
+        cob.append(same(w3col(ox, y_, c, out_w), cpart))
     mx.wait_recv()
-    co.wait_recv()
-    cob.wait_recv()
-
-    wo_all = wob[...].reshape(512, 1024)
-    middle = lat[...].astype(F32) + dot(jnp.concatenate([mix[0], mix[1]], axis=1), wo_all, NN)
+    for copy in cob:
+        copy.wait_recv()
+
+    middle = lat[...].astype(F32) + (dot(mix[0], weight(0, 3), NT) + dot(mix[1], weight(1, 3), NT))
     mid[...] = middle
     fmean = jnp.mean(middle, axis=-1, keepdims=True)
     fcen = middle - fmean
     frs = lax.rsqrt(jnp.mean(fcen * fcen, axis=-1, keepdims=True) + EPS)
     hid[r] = (fcen * frs * vec[4:5, :] + vec[5:6, :]).astype(BF16)
-    hids = [wire.send(hid.at[r], hid.at[r], (peer(k), j)) for k in (3, 2, 1)]
-
-    c3b = []
-    for copy, y_ in zip(x3, (yy, 1 - yy)):
-        copy.wait_recv()
-        c3b.append(same(w3col(ox, y_, c), cpart))
-    for copy in c3b:
-        copy.wait_recv()
-    attention(ox, False)
+    hids = wire.send_all([(hid.at[r], hid.at[r], (peer(k), j)) for k in (3, 2, 1)], hid.at[0:3])
 
     in_up.wait()
     in_dn.wait()
@@ -379,10 +375,8 @@
     for copy in dns:
         copy.wait_recv()
     cdn = same(dnb.at[c], cpart)
-    for copy in hids:
-        copy.wait_recv()
-    for copy in cots:
-        copy.wait_recv()
+    hids.wait_recv()
+    cots.wait_recv()
     cup.wait_recv()
     cdn.wait_recv()
 
@@ -398,23 +392,14 @@
     ig[...] = (agrad * (phi + inner * dens)).astype(BF16)
     hgs[...] = dot(ig[...], up_all, NT).astype(BF16).reshape(4, 64, 1024)
 
-    def reduce_sends(src, dst):
-        out = []
-        slot = x * 4 + r
-        for k in (7, 6, 5, 3, 2, 1, 4):
-            kx, kr = k // 4, k % 4
-            tx = ox if kx else x
-            tr = peer(kr) % 4
-            dev = (peer(kr), jx if kx else j)
-            out.append(wire.send(src.at[tr, at(tx * 32, 32), :], dst.at[slot], dev))
-        keep = pltpu.make_async_copy(
-            src.at[r, at(x * 32, 32), :], dst.at[slot], local_sem.at[len(local)]
-        )
-        keep.start()
-        local.append(keep)
-        return out, keep
-
-    hg_in, hg_keep = reduce_sends(hgs, hgr)
+    slot = x * 4 + r
+    parts = []
+    for k in (7, 6, 5, 3, 2, 1, 4):
+        tx, tj = (ox, jx) if k >= 4 else (x, j)
+        src = hgs.at[peer(k % 4) % 4, at(tx * 32, 32), :]
+        parts.append((src, hgr.at[slot], (peer(k % 4), tj)))
+    hg_in = wire.send_all(parts, hgr.at[0:7])
+    hgr[slot] = hgs[r, at(x * 32, 32), :]
 
     gus[...] = dot(hid_all, ig[:, at(oc * 256, 256)], TN).astype(BF16).reshape(8, 128, 256)
     gu_in = wire.send(gus, gur, cpart)
@@ -423,34 +408,44 @@
     guo[...] = dot(hid_all, ig[:, at(c * 256, 256)], TN).reshape(8, 128, 256)
     gdo[...] = dot(act[:, at(c * 256, 256)], cot_all, TN)
 
-    hg_keep.wait()
-    for copy in hg_in:
-        copy.wait_recv()
-
     def sum_of(ref, n):
         total = ref[0].astype(F32)
         for s in range(1, n):
             total = total + ref[s].astype(F32)
         return total
 
-    hgx[x] = sum_of(hgr, 8).astype(BF16)
-    hgx_in = same(hgx.at[x], xpart)
-
     fos[...] = dot(act[...], dn_all, NN).astype(BF16).reshape(4, 64, 1024)
+
+    def up_back(ks):
+        return wire.send_all([(gu.at[peer(k)], gua.at[i], (peer(k), j)) for k in ks], gua.at[0 : len(ks)])
+
+    def down_back(ks):
+        return wire.send_all(
+            [(gd.at[:, at(peer(k) * 128, 128)], gda.at[i], (peer(k), j)) for k in ks],
+            gda.at[0 : len(ks)],
+        )
+
     gu_in.wait_recv()
     gu[...] = (guo[...] + gur[...].astype(F32)).astype(BF16)
     gua[i] = gu[i]
-    gu_out = [wire.send(gu.at[peer(k)], gua.at[i], (peer(k), j)) for k in (4, 5, 6, 7, 1, 2, 3)]
+    gu_out = [up_back(near), up_back(crossing)]
     gd_in.wait_recv()
     gd[...] = (gdo[...] + gdr[...].astype(F32)).astype(BF16)
     gda[i] = gd[:, at(i * 128, 128)]
-    gd_out = [
-        wire.send(gd.at[:, at(peer(k) * 128, 128)], gda.at[i], (peer(k), j))
-        for k in (4, 5, 6, 7, 1, 2, 3)
-    ]
-
+    gd_out = [down_back(near)]
+    c3b = []
+    for copy, y_ in zip(x3, (yy, 1 - yy)):
+        copy.wait_recv()
+        c3b.append(same(w3col(ox, y_, c), cpart))
+    for copy in c3b:
+        copy.wait_recv()
+    attention(ox, False)
+
+    hg_in.wait_recv()
+    hgx[x] = sum_of(hgr, 8).astype(BF16)
+    hgx_in = same(hgx.at[x], xpart)
+    fx_in = wire.send(fos.at[:, at(ox * 32, 32), :], fxr, xpart)
     hgx_in.wait_recv()
-    fo_in, fo_keep = reduce_sends(fos, fors)
     dy = hgx[...].reshape(64, 1024).astype(F32)
     middle = mid[...]
     fmean = jnp.mean(middle, axis=-1, keepdims=True)
@@ -467,10 +462,8 @@
     middle_grad = cota[r].astype(F32) + dz
     midg[...] = middle_grad
     low = middle_grad.astype(BF16)
-    wo_all = wob[...].reshape(512, 1024)
-    mgr_all = dot(low, wo_all, NT).astype(BF16)
     for g in (0, 1):
-        mgr[g] = mgr_all[:, g * 256 : (g + 1) * 256]
+        mgr[g] = dot(low, weight(g, 3), NN).astype(BF16)
     lowb[...] = low
 
     def back_values(g):
@@ -498,25 +491,43 @@
             gown[ii // 2, ii % 2, m] = mine[:, cols]
             cgs[ii // 2, ii % 2, m] = other[:, cols].astype(BF16)
 
-    def two(ref, p):
-        return ref.at[:, :, 2 * p : 2 * p + 2]
+    def one(ref, p):
+        return ref.at[:, :, p]
 
     def chip_sum(p):
-        two(g1, p)[...] = (two(gown, p)[...] + two(cgr, p)[...].astype(F32)).astype(BF16)
-        return wire.send(g1.at[:, 1 - yy, 2 * p : 2 * p + 2], yr.at[:, 2 * p : 2 * p + 2], ypart)
+        one(g1, p)[...] = (one(gown, p)[...] + one(cgr, p)[...].astype(F32)).astype(BF16)
+        return wire.send(g1.at[:, 1 - yy, p], yr.at[:, p], ypart)
+
+    def to_core(p):
+        return wire.send(one(cgs, p), one(cgr, p), cpart)
 
     delta = back_values(x)
     split(0, dot(vg[x], kin[...], TN))
+    cg_in = [to_core(0)]
     split(1, dot(mix[x], lowb[...], TN))
-    cg_in = [wire.send(two(cgs, 0), two(cgr, 0), cpart)]
+    cg_in.append(to_core(1))
     back_keys(x, delta)
-    split(2, dot(kg[x], kin[...], TN))
-    split(3, dot(qg[x], kin[1280:1344, :], TN))
-    cg_in.append(wire.send(two(cgs, 1), two(cgr, 1), cpart))
     y_in = []
-    for p in (0, 1):
+
+    def to_y(p):
         cg_in[p].wait_recv()
         y_in.append(chip_sum(p))
+
+    to_y(0)
+    split(2, dot(kg[x], kin[...], TN))
+    cg_in.append(to_core(2))
+    to_y(1)
+    split(3, dot(qg[x], kin[1280:1344, :], TN))
+    cg_in.append(to_core(3))
+    to_y(2)
+    to_y(3)
+    fx_in.wait_recv()
+    fos2[...] = (fos[:, at(x * 32, 32), :].astype(F32) + fxr[...].astype(F32)).astype(BF16)
+    fors[r] = fos2[r]
+    fo_in = wire.send_all(
+        [(fos2.at[peer(k) % 4], fors.at[r], (peer(k), j)) for k in (3, 2, 1)], fors.at[0:3]
+    )
+    gd_out.append(down_back(crossing))
     back_keys(ox, back_values(ox))
 
     def dx_tile(rows):
@@ -533,13 +544,7 @@
 
     def out_copy(t, slot):
         rows = at(t * 256, 256)
-        return wire.make(slot, mgo.at[rows, :], media_out.at[c, rows, :], cpart)
-
-    def keep_copy(t):
-        rows = at(t * 256, 256)
-        return pltpu.make_async_copy(
-            mgo.at[rows, :], media_out.at[c, rows, :], local_sem.at[20 + t]
-        )
+        return wire.make(slot, media_out.at[c, rows, :], media_out.at[c, rows, :], cpart)
 
     def media_back(t, carry):
         dxs[0:256, :] = dx_tile(at(t * 256, 256))
@@ -548,100 +553,87 @@
         v = xin[rows, :].astype(F32)
         dy = dxs[0:256, :]
         dz, zhat = norm_back(v, mu[rows, :], rs[rows, :], vec[0:1, :], dy)
-        mgo[rows, :] = dz.astype(BF16)
+        media_out[c, rows, :] = dz.astype(BF16)
         accg[...] += (dy * zhat).reshape(32, 8, 1024).sum(0)
         accb[...] += dy.reshape(32, 8, 1024).sum(0)
         out_copy(t, out_base + t).start()
-        keep_copy(t).start()
         return carry
 
-    def pass_on(p):
+    zn, zf = peer(2) // 2, peer(4) // 2
+    zd = peer(6) // 2
+
+    def to_near(p):
         y_in[p].wait_recv()
-        here = slice(2 * p, 2 * p + 2)
-        g2[:, here] = (g1[:, yy, here].astype(F32) + yr[:, here].astype(F32)).astype(BF16)
-        zr[z, here] = g2[z, here]
-        return [
-            wire.send(g2.at[peer(2 * k) // 2, here], zr.at[z, here], (peer(2 * k), j))
-            for k in (2, 3, 1)
-        ]
-
-    lax.fori_loop(0, 1, media_back, 0)
-    z_in = pass_on(0)
-    lax.fori_loop(1, 3, media_back, 0)
-    z_in += pass_on(1)
-    lax.fori_loop(3, 5, media_back, 0)
+        g2[:, p] = (g1[:, yy, p].astype(F32) + yr[:, p].astype(F32)).astype(BF16)
+        parts = [(g2.at[zn, p], zr.at[0, p], (peer(2), j)), (g2.at[zd, p], zr.at[1, p], (peer(2), j))]
+        return wire.send_all(parts, zr.at[0:2, 0])
+
+    def to_far(p):
+        n_in[p].wait_recv()
+        zs[p] = (g2[zf, p].astype(F32) + zr[1, p].astype(F32)).astype(BF16)
+        return wire.send(zs.at[p], zr.at[2, p], (peer(4), j))
+
+    n_in, f_in = [], []
+    lax.fori_loop(0, 2, media_back, 0)
+    n_in.append(to_near(0))
+    lax.fori_loop(2, 4, media_back, 0)
+    n_in.append(to_near(1))
+    f_in.append(to_far(0))
+    lax.fori_loop(4, 5, media_back, 0)
     put_vec(0, jnp.sum(accg[...], axis=0, keepdims=True))
     put_vec(1, jnp.sum(accb[...], axis=0, keepdims=True))
     dxs[0:64, :] = dx_tile(pl.ds(1280, 64))
     lsum = dxs[0:64, :] + dot(qg[0], weight(0, 2), NT) + dot(qg[1], weight(1, 2), NT)
     lat32 = lat[...].astype(F32)
     dz, zhat = norm_back(lat32, mu[1280:1344, :], rs[1280:1344, :], vec[2:3, :], lsum)
-    outg[...] = (midg[...] + dz).astype(BF16)
-    lg_in = wire.send(outg, lgrad_out.at[c], cpart)
-    lg_keep = pltpu.make_async_copy(outg, lgrad_out.at[c], local_sem.at[25])
-    lg_keep.start()
+    lgrad_out[c] = (midg[...] + dz).astype(BF16)
+    lg_in = same(lgrad_out.at[c], cpart)
     put_vec(2, jnp.sum(lsum * zhat, axis=0, keepdims=True))
     put_vec(3, jnp.sum(lsum, axis=0, keepdims=True))
     for ii in range(8):
         vgs[ii, 6:8, :] = jnp.zeros((2, 128), F32)
     vg_in = wire.send(vgs, vgc, cpart)
 
+    n_in.append(to_near(2))
+    f_in.append(to_far(1))
+    fo_in.wait_recv()
+    fox[x] = sum_of(fors, 4).astype(BF16)
+    fox_in = same(fox.at[x], xpart)
+    n_in.append(to_near(3))
+    f_in.append(to_far(2))
     vg_in.wait_recv()
     vgt[...] = vgs[...] + vgc[...]
     vga[i] = vgt[i]
-    v_in = [wire.send(vgt.at[peer(k)], vga.at[i], (peer(k), j)) for k in range(1, 8)]
-
-    fo_keep.wait()
-    for copy in fo_in:
-        copy.wait_recv()
-    fox[x] = sum_of(fors, 8).astype(BF16)
-    fox_in = same(fox.at[x], xpart)
-
+    v_in = wire.send_all([(vgt.at[peer(k)], vga.at[i], (peer(k), j)) for k in others], vga.at[0:7])
+
+    fox_in.wait_recv()
+    lat_out[c] = (mid[...] + fox[...].reshape(64, 1024).astype(F32)).astype(BF16)
+    lo_in = same(lat_out.at[c], cpart)
+
+    f_in.append(to_far(3))
     for copy in gu_out:
         copy.wait_recv()
     for q in range(4):
-        gupv[:, q * 256 : (q + 1) * 256] = gua[q].astype(F32) + gua[4 + q].astype(F32)
-    gup_keep = pltpu.make_async_copy(gupv, gup, local_sem.at[27])
-    gup_keep.start()
+        gup[:, q * 256 : (q + 1) * 256] = gua[q].astype(F32) + gua[4 + q].astype(F32)
     for copy in gd_out:
         copy.wait_recv()
     for q in range(4):
-        gdnv[q * 256 : (q + 1) * 256, :] = gda[q].astype(F32) + gda[4 + q].astype(F32)
-    gdn_keep = pltpu.make_async_copy(gdnv, gdown, local_sem.at[28])
-    gdn_keep.start()
-
-    fox_in.wait_recv()
-    outl[...] = (mid[...] + fox[...].reshape(64, 1024).astype(F32)).astype(BF16)
-    lo_in = wire.send(outl, lat_out.at[c], cpart)
-    lo_keep = pltpu.make_async_copy(outl, lat_out.at[c], local_sem.at[26])
-    lo_keep.start()
-
-    for copy in z_in:
+        gdown[q * 256 : (q + 1) * 256, :] = gda[q].astype(F32) + gda[4 + q].astype(F32)
+
+    for copy in f_in:
         copy.wait_recv()
-    last = sum_of(zr, 4)
-    gmv[0] = last[3].T
-    gmv[1] = last[2].T
-    gmv[2] = last[0].T
-    gmv[3] = last[1]
-    gm_keep = pltpu.make_async_copy(gmv, gmat, local_sem.at[29])
-    gm_keep.start()
-    for copy in v_in:
-        copy.wait_recv()
-    vsum[...] = sum_of(vga, 8)
-    v_keep = pltpu.make_async_copy(vsum, vecs, local_sem.at[30])
-    v_keep.start()
+    last = g2[z].astype(F32) + zr[0].astype(F32) + zr[2].astype(F32)
+    gmat[0] = last[3].T
+    gmat[1] = last[2].T
+    gmat[2] = last[0].T
+    gmat[3] = last[1]
+    v_in.wait_recv()
+    vecs[...] = sum_of(vga, 8)
 
     for t in range(5):
-        keep_copy(t).wait()
         out = out_copy(t, out_base + t)
         out.wait_send()
         out.wait_recv()
-    lg_keep.wait()
-    lo_keep.wait()
-    gup_keep.wait()
-    gdn_keep.wait()
-    gm_keep.wait()
-    v_keep.wait()
     lg_in.wait_recv()
     lo_in.wait_recv()
     wire.drain()
@@ -656,8 +648,8 @@
     ("kin", (1344, 1024), BF16),
     ("mu", (1344, 1), F32),
     ("rs", (1344, 1), F32),
-    ("w3", (2, 4, 2, 3, 128, 256), BF16),
-    ("wob", (4, 128, 1024), BF16),
+    ("w4", (2, 4, 2, 4, 128, 256), BF16),
+    ("wo_own", (128, 128), BF16),
     ("upb", (8, 128, 512), BF16),
     ("dnb", (2, 256, 1024), BF16),
     ("kb", (2, 1344, 256), BF16),
@@ -675,7 +667,9 @@
     ("hgr", (8, 32, 1024), BF16),
     ("hgx", (2, 32, 1024), BF16),
     ("fos", (4, 64, 1024), BF16),
-    ("fors", (8, 32, 1024), BF16),
+    ("fxr", (4, 32, 1024), BF16),
+    ("fos2", (4, 32, 1024), BF16),
+    ("fors", (4, 32, 1024), BF16),
     ("fox", (2, 32, 1024), BF16),
     ("gus", (8, 128, 256), BF16),
     ("gur", (8, 128, 256), BF16),
@@ -699,18 +693,12 @@
     ("g1", (4, 2, 4, 128, 128), BF16),
     ("yr", (4, 4, 128, 128), BF16),
     ("g2", (4, 4, 128, 128), BF16),
-    ("zr", (4, 4, 128, 128), BF16),
+    ("zr", (3, 4, 128, 128), BF16),
+    ("zs", (4, 128, 128), BF16),
     ("dxs", (1344, 1024), F32),
     ("accg", (8, 1024), F32),
     ("accb", (8, 1024), F32),
-    ("mgo", (1280, 1024), BF16),
-    ("outl", (64, 1024), BF16),
-    ("outg", (64, 1024), BF16),
     ("wsc", (256, 1024), F32),
-    ("gupv", (128, 1024), F32),
-    ("gdnv", (1024, 128), F32),
-    ("gmv", (4, 128, 128), F32),
-    ("vsum", (8, 128), F32),
     ("vgs", (8, 8, 128), F32),
     ("vgc", (8, 8, 128), F32),
     ("vgt", (8, 8, 128), F32),
@@ -718,33 +706,15 @@
 )
 
 
-CHUNKS = 10
-
-
 def hand_out(lat, med, lgr, gmat, gup, gdown, vecs, *rest):
-    outs, (v_lat, v_med, v_lgr, v_gmat, v_gup, v_gdown, v_vecs, sem_in, sem_out) = rest[:15], rest[15:]
-    rows = med.shape[0] * med.shape[1] // CHUNKS
-    per = med.shape[1] // rows
-    moves = []
-    for k in range(CHUNKS):
-        part = (k // per, pl.ds((k % per) * rows, rows))
-        moves.append((med.at[part], v_med.at[part], [(v_med.at[part], outs[1].at[part])]))
-    moves.append((gup, v_gup, [(v_gup, outs[7])]))
-    moves.append((gdown, v_gdown, [(v_gdown, outs[8])]))
-    moves.append((lat, v_lat, [(v_lat, outs[0])]))
-    moves.append((lgr, v_lgr, [(v_lgr, outs[2])]))
-    moves.append((gmat, v_gmat, [(v_gmat.at[k], outs[3 + k]) for k in range(4)]))
-    moves.append((vecs, v_vecs, [(v_vecs.at[k : k + 1], outs[9 + k]) for k in range(6)]))
-    first = [pltpu.make_async_copy(a, b, sem_in.at[k]) for k, (a, b, _) in enumerate(moves)]
-    for copy in first:
+    outs, sem = rest[:15], rest[15]
+    moves = [(med, outs[1]), (gup, outs[7]), (gdown, outs[8]), (lat, outs[0]), (lgr, outs[2])]
+    moves += [(gmat.at[k], outs[3 + k]) for k in range(4)]
+    moves += [(vecs.at[k : k + 1], outs[9 + k]) for k in range(6)]
+    copies = [pltpu.make_async_copy(a, b, sem.at[k]) for k, (a, b) in enumerate(moves)]
+    for copy in copies:
         copy.start()
-    second = []
-    for copy, (_, _, then) in zip(first, moves):
-        copy.wait()
-        for a, b in then:
-            second.append(pltpu.make_async_copy(a, b, sem_out.at[len(second)]))
-            second[-1].start()
-    for copy in second:
+    for copy in copies:
         copy.wait()
 
 
@@ -756,24 +726,24 @@
     outs = pl.pallas_call(
         layer_kernel,
         out_shape=[
-            shape(latents.shape, BF16),
-            shape(media.shape, BF16),
-            shape(latents.shape, BF16),
-            shape((4, 128, 128), F32),
-            shape(up.shape, F32),
-            shape(down.shape, F32),
-            shape((8, 128), F32),
+            pltpu.VMEM(latents.shape, BF16),
+            pltpu.VMEM(media.shape, BF16),
+            pltpu.VMEM(latents.shape, BF16),
+            pltpu.VMEM((4, 128, 128), F32),
+            pltpu.VMEM(up.shape, F32),
+            pltpu.VMEM(down.shape, F32),
+            pltpu.VMEM((8, 128), F32),
         ],
         in_specs=[smem] + [anyspace] * 9 + [vmem] * 6,
-        out_specs=[anyspace] * 7,
+        out_specs=[vmem] * 7,
         scratch_shapes=[
             pltpu.SemaphoreType.DMA((SEMS,)),
             pltpu.SemaphoreType.DMA((SEMS,)),
-            pltpu.SemaphoreType.DMA((32,)),
+            pltpu.SemaphoreType.DMA((9,)),
         ]
         + [pltpu.VMEM(size, kind) for _, size, kind in SCRATCH],
         compiler_params=pltpu.CompilerParams(
-            collective_id=0, has_side_effects=True, vmem_limit_bytes=60 * 2**20
+            collective_id=0, has_side_effects=True, vmem_limit_bytes=LIMIT * 2**20
         ),
         cost_estimate=pl.CostEstimate(
             flops=14 * 10**9, bytes_accessed=20 * 10**6, transcendentals=10**6
@@ -793,15 +763,14 @@
     )
     outs = pl.pallas_call(
         hand_out,
-        out_shape=[shape(v.shape, v.dtype) for v in outs[:3]]
+        out_shape=[shape(v.shape, BF16) for v in (latents, media, latents)]
         + [shape(v.shape, F32) for v in (wq, wk, wv, wo, up, down)]
         + [shape((1, 128), F32)] * 6,
-        in_specs=[anyspace] * 7,
+        in_specs=[vmem] * 7,
         out_specs=[anyspace] * 15,
-        scratch_shapes=[pltpu.VMEM(v.shape, v.dtype) for v in outs]
-        + [pltpu.SemaphoreType.DMA((CHUNKS + 6,)), pltpu.SemaphoreType.DMA((CHUNKS + 14,))],
-        compiler_params=pltpu.CompilerParams(vmem_limit_bytes=60 * 2**20),
-    )(*outs)
+        scratch_shapes=[pltpu.SemaphoreType.DMA((15,))],
+        compiler_params=pltpu.CompilerParams(vmem_limit_bytes=4 * 2**20),
+    )(*[pltpu.with_memory_space_constraint(v, pltpu.VMEM) for v in outs])
     return tuple(outs[:9]) + tuple(v.reshape(128) for v in outs[9:])
 
 

time: 107 us -> 100 us (0.935)
  Pallas kernels: 106 us -> 99.2 us
    pallas_call x2, Pallas kernels: 106 us -> 99.2 us  [the longest x1 96.2 us: fused(): pl.pallas_call(layer_kernel, out_shape=[pltpu.VMEM(latents.shape, BF16),...]
where the time goes in v3:
time: 100 us
  Pallas kernels  99.2 us (99%)
    pallas_call x1, Pallas kernels, fused(): pl.pallas_call(layer_kernel, out_shape=[pltpu.VMEM(latents.shape, BF16),...  96.2 us
    pallas_call x1, Pallas kernels, fused(): pl.pallas_call(hand_out, out_shape=[shape(v.shape, BF16) for v in (latent...  3.04 us

profile of v3, /device:TPU:0, one launch (start us, length us, event | category | flops | bytes accessed | tf_op | source)
XLA Modules:
  0.0 100.0 jit_solution(12422019827369928714)
XLA Ops:
  0.7 96.2 %shard_map.271 = (bf16[2,64,1024]{2,1,0:T(8,128)(2,1)S(1)}, bf16[2,1280,1024]{2,1,0:T(8,128)(2,1)S(1)}, bf16[2,64,1024]{2,1,0:T(8,128)(2,1)S(1)}, f32[4,128,128]...) custom-call(s32[2]{0:T(128)} %counts.1, ...), custom_call_target="tpu_custom_call" | custom-call | flops 14000000000 | bytes 20000000 | tf_op jit(solution)/shard_map/pallas_call | solution.py:726
  96.8 3.0 %shard_map.272 = (bf16[2,64,1024]{2,1,0:T(8,128)(2,1)}, bf16[2,1280,1024]{2,1,0:T(8,128)(2,1)}, bf16[2,64,1024]{2,1,0:T(8,128)(2,1)}, f32[128,128]{1,0:T(8,128)}...) custom-call(bf16[2,64,1024]{2,1,0:T(8,128)(2,1)S(1)} %get-tuple-elem, ...), custom_call_target="tpu_custom_call" | custom-call | tf_op jit(solution)/shard_map/pallas_call | solution.py:764

commit v4 on v3

--- a/solution.py
+++ b/solution.py
@@ -17,7 +17,7 @@
 NT = (((1,), (1,)), ((), ()))
 TN = (((0,), (0,)), ((), ()))
 LIMIT = 54
-SEMS = 68
+SEMS = 70
 
 
 def dot(a, b, dims):
@@ -285,6 +285,11 @@
     c3 = [same(w3col(x, yy, c, everything), cpart)]
     xo = [same(w3col(x, yy, c, out_w), xpart)]
     x3 = [same(w3col(x, yy, c), xpart)]
+    in_cot.wait()
+    half = at(x * 32, 32)
+    cots = wire.send_all(
+        [(cota.at[r, half], cota.at[r, half], (peer(k), j)) for k in (3, 2, 1)], cota.at[0:3, 0:32]
+    )
     def up_part(k):
         return up.at[:, at(peer(k) % 4 * 256, 256)], upb.at[i, :, at(c * 256, 256)], (peer(k), j)
 
@@ -296,11 +301,6 @@
     dns = [wire.send_all([down_part(k) for k in near], dnb.at[0, :, 0:384])]
     ups.append(wire.send_all([up_part(k) for k in crossing], upb.at[0:4, :, 0:256]))
     dns.append(wire.send_all([down_part(k) for k in crossing], dnb.at[0, :, 0:512]))
-    in_cot.wait()
-    cots = wire.send_all(
-        [(cota.at[r], cota.at[r], (peer(k), j)) for k in (1, 2, 3)], cota.at[0:3]
-    )
-
     media_norm(10, 20)
     for copy in y3:
         copy.wait_recv()
@@ -350,6 +350,9 @@
 
     attention(x)
     mx = same(mix.at[x], xpart)
+    cots.wait_recv()
+    halves = [cota.at[peer(k) % 4, half] for k in (3, 2, 1)]
+    cots_x = wire.send_all([(v, v, xpart) for v in halves], cota.at[0:3, 0:32])
     x3.append(same(w3col(x, 1 - yy, c), xpart))
     cob = []
     for copy, y_ in zip(xo, (yy, 1 - yy)):
@@ -376,7 +379,7 @@
         copy.wait_recv()
     cdn = same(dnb.at[c], cpart)
     hids.wait_recv()
-    cots.wait_recv()
+    cots_x.wait_recv()
     cup.wait_recv()
     cdn.wait_recv()
 
@@ -578,8 +581,9 @@
     n_in.append(to_near(0))
     lax.fori_loop(2, 4, media_back, 0)
     n_in.append(to_near(1))
+    lax.fori_loop(4, 5, media_back, 0)
     f_in.append(to_far(0))
-    lax.fori_loop(4, 5, media_back, 0)
+    n_in.append(to_near(2))
     put_vec(0, jnp.sum(accg[...], axis=0, keepdims=True))
     put_vec(1, jnp.sum(accb[...], axis=0, keepdims=True))
     dxs[0:64, :] = dx_tile(pl.ds(1280, 64))
@@ -594,22 +598,16 @@
         vgs[ii, 6:8, :] = jnp.zeros((2, 128), F32)
     vg_in = wire.send(vgs, vgc, cpart)
 
-    n_in.append(to_near(2))
     f_in.append(to_far(1))
-    fo_in.wait_recv()
-    fox[x] = sum_of(fors, 4).astype(BF16)
-    fox_in = same(fox.at[x], xpart)
     n_in.append(to_near(3))
-    f_in.append(to_far(2))
     vg_in.wait_recv()
     vgt[...] = vgs[...] + vgc[...]
     vga[i] = vgt[i]
     v_in = wire.send_all([(vgt.at[peer(k)], vga.at[i], (peer(k), j)) for k in others], vga.at[0:7])
-
-    fox_in.wait_recv()
-    lat_out[c] = (mid[...] + fox[...].reshape(64, 1024).astype(F32)).astype(BF16)
-    lo_in = same(lat_out.at[c], cpart)
-
+    f_in.append(to_far(2))
+    fo_in.wait_recv()
+    fox[x] = sum_of(fors, 4).astype(BF16)
+    fox_in = same(fox.at[x], xpart)
     f_in.append(to_far(3))
     for copy in gu_out:
         copy.wait_recv()
@@ -620,6 +618,9 @@
     for q in range(4):
         gdown[q * 256 : (q + 1) * 256, :] = gda[q].astype(F32) + gda[4 + q].astype(F32)
 
+    fox_in.wait_recv()
+    lat_out[c] = (mid[...] + fox[...].reshape(64, 1024).astype(F32)).astype(BF16)
+    lo_in = same(lat_out.at[c], cpart)
     for copy in f_in:
         copy.wait_recv()
     last = g2[z].astype(F32) + zr[0].astype(F32) + zr[2].astype(F32)

time: 100 us -> 98.4 us (0.984)
  Pallas kernels: 99.2 us -> 97.4 us
    pallas_call x1, Pallas kernels: 96.2 us -> 94.4 us  [fused(): pl.pallas_call(layer_kernel, out_shape=[pltpu.VMEM(latents.shape, BF16),...]
where the time goes in v4:
time: 98.4 us; the launch traced here: 98.2 us
  Pallas kernels  97.4 us (99%)
    pallas_call x1, Pallas kernels, fused(): pl.pallas_call(layer_kernel, out_shape=[pltpu.VMEM(latents.shape, BF16),...  94.4 us
    pallas_call x1, Pallas kernels, fused(): pl.pallas_call(hand_out, out_shape=[shape(v.shape, BF16) for v in (latent...  3.04 us

profile of v4, /device:TPU:0, one launch (start us, length us, event | category | flops | bytes accessed | tf_op | source)
XLA Modules:
  0.0 98.2 jit_solution(16176314586242542003)
XLA Ops:
  0.7 94.4 %shard_map.271 = (bf16[2,64,1024]{2,1,0:T(8,128)(2,1)S(1)}, bf16[2,1280,1024]{2,1,0:T(8,128)(2,1)S(1)}, bf16[2,64,1024]{2,1,0:T(8,128)(2,1)S(1)}, f32[4,128,128]...) custom-call(s32[2]{0:T(128)} %counts.1, ...), custom_call_target="tpu_custom_call" | custom-call | flops 14000000000 | bytes 20000000 | tf_op jit(solution)/shard_map/pallas_call | solution.py:727
  95.0 3.0 %shard_map.272 = (bf16[2,64,1024]{2,1,0:T(8,128)(2,1)}, bf16[2,1280,1024]{2,1,0:T(8,128)(2,1)}, bf16[2,64,1024]{2,1,0:T(8,128)(2,1)}, f32[128,128]{1,0:T(8,128)}...) custom-call(bf16[2,64,1024]{2,1,0:T(8,128)(2,1)S(1)} %get-tuple-elem, ...), custom_call_target="tpu_custom_call" | custom-call | tf_op jit(solution)/shard_map/pallas_call | solution.py:765

commit v5 on v4

--- a/solution.py
+++ b/solution.py
@@ -297,15 +297,15 @@
         return down.at[at(peer(k) % 4 * 256, 256), :], dnb.at[c, :, at(i * 128, 128)], (peer(k), j)
 
     near, crossing = (4, 6, 2), (5, 7, 3, 1)
-    ups = [wire.send_all([up_part(k) for k in near], upb.at[0:3, :, 0:256])]
-    dns = [wire.send_all([down_part(k) for k in near], dnb.at[0, :, 0:384])]
-    ups.append(wire.send_all([up_part(k) for k in crossing], upb.at[0:4, :, 0:256]))
-    dns.append(wire.send_all([down_part(k) for k in crossing], dnb.at[0, :, 0:512]))
+    ups = [wire.send_all([up_part(k) for k in near[:2]], upb.at[0:2, :, 0:256])]
+    dns = [wire.send_all([down_part(k) for k in near[:2]], dnb.at[0, :, 0:256])]
     media_norm(10, 20)
     for copy in y3:
         copy.wait_recv()
     c3.append(same(w3col(x, 1 - yy, c, everything), cpart))
     xo.append(same(w3col(x, 1 - yy, c, out_w), xpart))
+    ups.append(wire.send_all([up_part(k) for k in (5, 7, 2, 3, 1)], upb.at[0:5, :, 0:256]))
+    dns.append(wire.send_all([down_part(k) for k in (5, 7, 2, 3, 1)], dnb.at[0, :, 0:640]))
     for copy in c3:
         copy.wait_recv()
 

time: 98.4 us -> 98.2 us (level)
  no operation moved by 1% of the time
where the time goes in v5:
time: 98.2 us; the launch traced here: 98 us
  Pallas kernels  97.2 us (99%)
    pallas_call x1, Pallas kernels, fused(): pl.pallas_call(layer_kernel, out_shape=[pltpu.VMEM(latents.shape, BF16),...  94.1 us
    pallas_call x1, Pallas kernels, fused(): pl.pallas_call(hand_out, out_shape=[shape(v.shape, BF16) for v in (latent...  3.04 us

profile of v5, /device:TPU:0, one launch (start us, length us, event | category | flops | bytes accessed | tf_op | source)
XLA Modules:
  0.0 98.0 jit_solution(3431059055972580143)
XLA Ops:
  0.7 94.1 %shard_map.271 = (bf16[2,64,1024]{2,1,0:T(8,128)(2,1)S(1)}, bf16[2,1280,1024]{2,1,0:T(8,128)(2,1)S(1)}, bf16[2,64,1024]{2,1,0:T(8,128)(2,1)S(1)}, f32[4,128,128]...) custom-call(s32[2]{0:T(128)} %counts.1, ...), custom_call_target="tpu_custom_call" | custom-call | flops 14000000000 | bytes 20000000 | tf_op jit(solution)/shard_map/pallas_call | solution.py:727
  94.8 3.0 %shard_map.272 = (bf16[2,64,1024]{2,1,0:T(8,128)(2,1)}, bf16[2,1280,1024]{2,1,0:T(8,128)(2,1)}, bf16[2,64,1024]{2,1,0:T(8,128)(2,1)}, f32[128,128]{1,0:T(8,128)}...) custom-call(bf16[2,64,1024]{2,1,0:T(8,128)(2,1)S(1)} %get-tuple-elem, ...), custom_call_target="tpu_custom_call" | custom-call | tf_op jit(solution)/shard_map/pallas_call | solution.py:765
